TPU v7x, 128 devices: a whole 4x4x4 slice. The times are simulated.
128 devices in a mesh: ctx: 16 (over y, z), tp: 8 (over x, core).
Axes of the slice: x: 4, y: 4, z: 4, core: 2. Of those that a mesh axis runs over, the one named last changes fastest.
Arguments:
- mamba_input: bfloat16 [16384, 16384], P('ctx', 'tp'), may hold values from -6 to 6
- conv_weight: float32 [4, 16384], P(None, 'tp'), may hold values from -3 to 3
- mamba_gate: bfloat16 [16384, 16384], P('ctx', 'tp'), may hold values from -6 to 6
- state_write: bfloat16 [16384, 1024], P('ctx', 'tp'), may hold values from -1 to 1
- state_read: bfloat16 [16384, 1024], P('ctx', 'tp'), may hold values from -6 to 6
- step_size: float32 [256, 16384], P('tp', 'ctx'), may hold values from 0 to 10
- log_decay: float32 [256, 16384], P('tp', 'ctx'), may hold values from -1 to 0
- skip_gain: float32 [256], P('tp'), may hold values from 0.5 to 1.5
- norm_gain: float32 [16384], P('tp'), may hold values from 0.1 to 1.9
Outputs:
- mamba_out: bfloat16 [16384, 16384], P('ctx', 'tp')
All inputs are finite; a program needn't handle non-finite values.
Results may differ from a plain program's by a relative error of at most 0.001.
Values may be sent and summed in bfloat16 or wider, within the bound.
No kernel may reach another device: no remote copies, remote signals or barrier semaphores. Data moves between devices by JAX's collectives and lax.ppermute only.
A program may use at most 128 MiB of HBM per device.

v0:
```python
import jax
import jax.numpy as jnp
from jax import lax
from jax.sharding import PartitionSpec as P

MDIM = 64
STATE = 128
CONV = 4
SPAN = 128


def shifted(value, axis, steps):
    count = lax.axis_size(axis)
    initial, last = (max(0, -steps), min(count, count - steps))
    return lax.ppermute(value, axis, [(source, source + steps) for source in range(initial, last)])


def span_step(carried, inputs):
    input_blk, step_blk, decay_blk, write_blk, read_blk = inputs
    length, ngroup, group_width = input_blk.shape
    state_dim = write_blk.shape[2]
    hwidth = MDIM
    per_group = group_width // hwidth
    nheads = ngroup * per_group
    running = jnp.cumsum(decay_blk, axis=0)
    causal_mask = (lax.iota(jnp.int32, length)[:, None] >= lax.iota(jnp.int32, length)[None, :])[
        :, :, None
    ]
    decay_gap = jnp.where(causal_mask, running[:, None, :] - running[None, :, :], 0.0)
    fading = jnp.where(causal_mask, jnp.exp(decay_gap), 0.0).reshape(
        length, length, ngroup, per_group
    )
    intersection = jnp.einsum(
        "tgn,sgn->tsg", read_blk, write_blk, preferred_element_type=jnp.float32
    )
    scaled = step_blk.reshape(length, ngroup, per_group)
    mixing = fading * intersection[:, :, :, None] * scaled[None, :, :, :]
    input_grp = input_blk.reshape(length, ngroup, per_group, hwidth)
    within = jnp.einsum("tsgh,sghp->tghp", mixing, input_grp, precision=lax.Precision.HIGHEST)
    state_grp = carried.reshape(ngroup, per_group, hwidth, state_dim)
    across = jnp.exp(running).reshape(length, ngroup, per_group)[:, :, :, None] * jnp.einsum(
        "tgn,ghpn->tghp", read_blk.astype(jnp.float32), state_grp, precision=lax.Precision.HIGHEST
    )
    tail_weight = (jnp.exp(running[-1][None, :] - running) * step_blk).reshape(
        length, ngroup, per_group
    )
    weighted = tail_weight[:, :, :, None] * input_grp
    incoming = jnp.einsum(
        "sghp,sgn->ghpn", weighted, write_blk.astype(jnp.float32), precision=lax.Precision.HIGHEST
    )
    new_state = jnp.exp(running[-1])[:, None, None] * carried + incoming.reshape(
        nheads, hwidth, state_dim
    )
    return (new_state, (within + across).reshape(length, nheads, hwidth))


def run_spans(input_rows, step_rows, decay_rows, write_rows, read_rows, initial):
    pieces = input_rows.shape[0] // SPAN

    def fold_rows(array):
        return array.reshape((pieces, SPAN) + array.shape[1:])

    final, outputs = lax.scan(
        span_step,
        initial,
        (
            fold_rows(input_rows),
            fold_rows(step_rows),
            fold_rows(decay_rows),
            fold_rows(write_rows),
            fold_rows(read_rows),
        ),
    )
    return (final, outputs.reshape((input_rows.shape[0],) + outputs.shape[2:]))


def gated_norm(outputs, input_rows, gate_in, skip_gain, norm_gain, ngroup):
    ssm_total = outputs + skip_gain[None, :, None] * input_rows
    gated = ssm_total * jax.nn.silu(gate_in.astype(jnp.float32).reshape(input_rows.shape))
    token_count = input_rows.shape[0]
    grouped = gated.reshape(token_count, ngroup, -1)
    inverse = lax.rsqrt(jnp.mean(grouped * grouped, axis=-1, keepdims=True) + 1e-05)
    normed = grouped * inverse * norm_gain.reshape(ngroup, -1)[None, :, :]
    return normed.astype(jnp.bfloat16).reshape(token_count, -1)


def shards(
    mamba_input,
    conv_weight,
    mamba_gate,
    state_write,
    state_read,
    step_size,
    log_decay,
    skip_gain,
    norm_gain,
):
    tokens = mamba_input.shape[0]
    earlier_rows = shifted(mamba_input[tokens - (CONV - 1) :], "ctx", 1)
    padded = jnp.concatenate(
        [earlier_rows.astype(jnp.float32), mamba_input.astype(jnp.float32)], axis=0
    )
    total = jnp.zeros(mamba_input.shape, jnp.float32)
    for tap in range(CONV):
        total = total + conv_weight[tap][None, :] * padded[tap : tap + tokens]
    conv_in = jax.nn.silu(total)
    ngroup = state_write.shape[1] // STATE
    nheads = mamba_input.shape[1] // MDIM
    per_group = nheads // ngroup
    input_grouped = conv_in.reshape(tokens, ngroup, per_group * MDIM)
    write_rows = state_write.reshape(tokens, ngroup, STATE)
    read_rows = state_read.reshape(tokens, ngroup, STATE)
    decay_rows = log_decay.T
    zero_state = jnp.zeros((nheads, MDIM, STATE), jnp.float32)
    end_state, outputs = run_spans(
        input_grouped, step_size.T, decay_rows, write_rows, read_rows, zero_state
    )
    running = jnp.cumsum(decay_rows, axis=0)
    total_decay = jnp.exp(running[-1])

    def relay_state(turn_number, entering):
        return shifted(total_decay[:, None, None] * entering + end_state, "ctx", 1)

    entering = lax.fori_loop(0, lax.axis_size("ctx") - 1, relay_state, zero_state)
    reach = jnp.einsum(
        "tgn,ghpn->tghp",
        read_rows.astype(jnp.float32),
        entering.reshape(ngroup, per_group, MDIM, STATE),
        precision=lax.Precision.HIGHEST,
    )
    outputs = outputs + (
        jnp.exp(running).reshape(tokens, ngroup, per_group)[:, :, :, None] * reach
    ).reshape(tokens, nheads, MDIM)
    input_rows = conv_in.reshape(tokens, nheads, MDIM)
    return gated_norm(outputs, input_rows, mamba_gate, skip_gain, norm_gain, ngroup)


def solution(mesh):
    placed = (
        P("ctx", "tp"),
        P(None, "tp"),
        P("ctx", "tp"),
        P("ctx", "tp"),
        P("ctx", "tp"),
        P("tp", "ctx"),
        P("tp", "ctx"),
        P("tp"),
        P("tp"),
    )
    return jax.shard_map(
        shards, mesh=mesh, in_specs=placed, out_specs=P("ctx", "tp"), check_vma=False
    )
```

profile of v0, /device:TPU:22, one launch (start us, length us, event | category | flops | bytes accessed | tf_op | source)
XLA Modules:
  0.0 811.3 jit_solution(2485239239716891828)
XLA Ops:
  1.1 3.8 collective-permute-start.1
  5.9 9.0 %reduce-window.6 = f32[32,8,128]{2,1,0:T(8,128)S(1)} reduce-window(f32[32,8,128]{2,1,0:T(8,128)S(1)} %bitcast.152, f32[]{:T(128)} %constant.39.clone.1), window={size=1x1x128 pad=0_0x0_0x127_0}, to_apply=%region_3.4 | reduce-window | flops 4161536 | bytes 262148 | tf_op jit(solution)/shard_map/reduce-window
  17.7 6.4 copy.66
  24.1 6.5 convert_element_type.17
  32.6 6.4 copy.71
  39.8 18.7 %divide_multiply_fusion = f32[1024,2048]{0,1:T(8,128)S(1)} fusion(f32[1024,2048]{0,1:T(8,128)} %convert_element_type.17, f32[3,2048]{0,1:T(8,128)S(1)} %convert_element_type.16, f32[2048]{0:T(1024)S(1)} %bitcast.157, f32[2048]{0:T(1024)S(1)} %bitcast.158, f32[2048]{0:T(1024)S(1)} %bitcast.156, f32[2048]{0:T(1024)S(1)} %bitcast.155), kind=kLoop, calls=%fused_computation.67 | loop fusion | flops 29360128 | bytes 16834560 | tf_op jit(solution)/shard_map/jit(silu)/mul | solution.py:106
  58.5 5.7 copy.79
  64.2 349.6 %while.24 = (s32[]{:T(128)}, f32[32,64,128]{2,1,0:T(8,128)S(1)}, f32[8,128,32,64]{1,0,3,2:T(8,128)}, f32[8,128,32]{2,1,0:T(8,128)}, f32[8,128,32]{2,1,0:T(8,128)...) while((s32[]{:T(128)}, f32[32,64,128]{2,1,0:T(8,128)S(1)}, ...), condition=%wide.region_2.3_spmd.clone, body=%wide.region_0.2_spmd.clone.sunk | while | flops 1217155072 | bytes 17549712 | solution.py:63
  67.3 3.9 constant_dynamic-slice_fusion.2
  71.2 5.3 fusion.76
  78.4 27.3 %dynamic_update_slice.6 = f32[8,128,32,64]{1,0,3,2:T(8,128)} dynamic-update-slice(f32[8,128,32,64]{1,0,3,2:T(8,128)} %get-tuple-element.258, f32[1,128,32,64]{1,0,3,2:T(1,128)S(1)} %bitcast.142, s32[]{:T(128)} %get-tuple-element.256, s32[]{:T(128)} %constant.38.clone.1..sunk, s32[]{:T(128)} %constant.38.clone.1..sunk, s32[]{:T(128)} %constant.38.clone.1..sunk) | dynamic-update-slice | bytes 2097156 | tf_op jit(solution)/shard_map/while/body/jit(dynamic_update_index_in_dim)/dynamic_update_slice | solution.py:63
  111.0 3.9 constant_dynamic-slice_fusion.2
  114.9 5.3 fusion.76
  122.2 27.3 %dynamic_update_slice.6 = f32[8,128,32,64]{1,0,3,2:T(8,128)} dynamic-update-slice(f32[8,128,32,64]{1,0,3,2:T(8,128)} %get-tuple-element.258, f32[1,128,32,64]{1,0,3,2:T(1,128)S(1)} %bitcast.142, s32[]{:T(128)} %get-tuple-element.256, s32[]{:T(128)} %constant.38.clone.1..sunk, s32[]{:T(128)} %constant.38.clone.1..sunk, s32[]{:T(128)} %constant.38.clone.1..sunk) | dynamic-update-slice | bytes 2097156 | tf_op jit(solution)/shard_map/while/body/jit(dynamic_update_index_in_dim)/dynamic_update_slice | solution.py:63
  154.7 3.9 constant_dynamic-slice_fusion.2
  158.6 5.3 fusion.76
  165.9 27.3 %dynamic_update_slice.6 = f32[8,128,32,64]{1,0,3,2:T(8,128)} dynamic-update-slice(f32[8,128,32,64]{1,0,3,2:T(8,128)} %get-tuple-element.258, f32[1,128,32,64]{1,0,3,2:T(1,128)S(1)} %bitcast.142, s32[]{:T(128)} %get-tuple-element.256, s32[]{:T(128)} %constant.38.clone.1..sunk, s32[]{:T(128)} %constant.38.clone.1..sunk, s32[]{:T(128)} %constant.38.clone.1..sunk) | dynamic-update-slice | bytes 2097156 | tf_op jit(solution)/shard_map/while/body/jit(dynamic_update_index_in_dim)/dynamic_update_slice | solution.py:63
  198.4 3.9 constant_dynamic-slice_fusion.2
  202.3 5.3 fusion.76
  209.6 27.3 %dynamic_update_slice.6 = f32[8,128,32,64]{1,0,3,2:T(8,128)} dynamic-update-slice(f32[8,128,32,64]{1,0,3,2:T(8,128)} %get-tuple-element.258, f32[1,128,32,64]{1,0,3,2:T(1,128)S(1)} %bitcast.142, s32[]{:T(128)} %get-tuple-element.256, s32[]{:T(128)} %constant.38.clone.1..sunk, s32[]{:T(128)} %constant.38.clone.1..sunk, s32[]{:T(128)} %constant.38.clone.1..sunk) | dynamic-update-slice | bytes 2097156 | tf_op jit(solution)/shard_map/while/body/jit(dynamic_update_index_in_dim)/dynamic_update_slice | solution.py:63
  242.1 3.9 constant_dynamic-slice_fusion.2
  246.0 5.3 fusion.76
  253.3 27.3 %dynamic_update_slice.6 = f32[8,128,32,64]{1,0,3,2:T(8,128)} dynamic-update-slice(f32[8,128,32,64]{1,0,3,2:T(8,128)} %get-tuple-element.258, f32[1,128,32,64]{1,0,3,2:T(1,128)S(1)} %bitcast.142, s32[]{:T(128)} %get-tuple-element.256, s32[]{:T(128)} %constant.38.clone.1..sunk, s32[]{:T(128)} %constant.38.clone.1..sunk, s32[]{:T(128)} %constant.38.clone.1..sunk) | dynamic-update-slice | bytes 2097156 | tf_op jit(solution)/shard_map/while/body/jit(dynamic_update_index_in_dim)/dynamic_update_slice | solution.py:63
  285.8 3.9 constant_dynamic-slice_fusion.2
  289.7 5.3 fusion.76
  297.0 27.3 %dynamic_update_slice.6 = f32[8,128,32,64]{1,0,3,2:T(8,128)} dynamic-update-slice(f32[8,128,32,64]{1,0,3,2:T(8,128)} %get-tuple-element.258, f32[1,128,32,64]{1,0,3,2:T(1,128)S(1)} %bitcast.142, s32[]{:T(128)} %get-tuple-element.256, s32[]{:T(128)} %constant.38.clone.1..sunk, s32[]{:T(128)} %constant.38.clone.1..sunk, s32[]{:T(128)} %constant.38.clone.1..sunk) | dynamic-update-slice | bytes 2097156 | tf_op jit(solution)/shard_map/while/body/jit(dynamic_update_index_in_dim)/dynamic_update_slice | solution.py:63
  329.5 3.9 constant_dynamic-slice_fusion.2
  333.4 5.3 fusion.76
  340.7 27.3 %dynamic_update_slice.6 = f32[8,128,32,64]{1,0,3,2:T(8,128)} dynamic-update-slice(f32[8,128,32,64]{1,0,3,2:T(8,128)} %get-tuple-element.258, f32[1,128,32,64]{1,0,3,2:T(1,128)S(1)} %bitcast.142, s32[]{:T(128)} %get-tuple-element.256, s32[]{:T(128)} %constant.38.clone.1..sunk, s32[]{:T(128)} %constant.38.clone.1..sunk, s32[]{:T(128)} %constant.38.clone.1..sunk) | dynamic-update-slice | bytes 2097156 | tf_op jit(solution)/shard_map/while/body/jit(dynamic_update_index_in_dim)/dynamic_update_slice | solution.py:63
  373.2 3.9 constant_dynamic-slice_fusion.2
  377.1 5.3 fusion.76
  384.4 27.3 %dynamic_update_slice.6 = f32[8,128,32,64]{1,0,3,2:T(8,128)} dynamic-update-slice(f32[8,128,32,64]{1,0,3,2:T(8,128)} %get-tuple-element.258, f32[1,128,32,64]{1,0,3,2:T(1,128)S(1)} %bitcast.142, s32[]{:T(128)} %get-tuple-element.256, s32[]{:T(128)} %constant.38.clone.1..sunk, s32[]{:T(128)} %constant.38.clone.1..sunk, s32[]{:T(128)} %constant.38.clone.1..sunk) | dynamic-update-slice | bytes 2097156 | tf_op jit(solution)/shard_map/while/body/jit(dynamic_update_index_in_dim)/dynamic_update_slice | solution.py:63
  414.0 373.3 %while.23 = (s32[]{:T(128)}, f32[32,64,128]{2,1,0:T(8,128)S(1)}, f32[32]{0:T(128)}, f32[32,64,128]{2,1,0:T(8,128)S(1)}, s32[]{:T(128)}) while((s32[]{:T(128)}, f32[32,64,128]{2,1,0:T(8,128)S(1)}, f32[32]{0:T(128)}, f32[32,64,128]{2,1,0:T(8,128)S(1)}, s32[]{:T(128)}) %tuple.50), condition=%wide.region_6.7_spmd, body=%wide.region_5.6_spmd.sunk | while | flops 524290 | bytes 7340261 | solution.py:124
  414.8 3.8 collective-permute-start
  418.6 24.8 %collective-permute-done = f32[32,64,128]{2,1,0:T(8,128)S(1)} collective-permute-done((f32[32,64,128]{2,1,0:T(8,128)S(1)}, f32[32,64,128]{2,1,0:T(8,128)S(1)}, u32[]{:S(2)}, u32[]{:S(2)}) %collective-permute-start) | collective-permute-done | bytes 1048608 | tf_op jit(solution)/shard_map/while/body/eval_jaxpr/ppermute | solution.py:15
  444.2 1.9 collective-permute-start
  446.1 25.8 %collective-permute-done = f32[32,64,128]{2,1,0:T(8,128)S(1)} collective-permute-done((f32[32,64,128]{2,1,0:T(8,128)S(1)}, f32[32,64,128]{2,1,0:T(8,128)S(1)}, u32[]{:S(2)}, u32[]{:S(2)}) %collective-permute-start) | collective-permute-done | bytes 1048608 | tf_op jit(solution)/shard_map/while/body/eval_jaxpr/ppermute | solution.py:15
  472.7 1.9 collective-permute-start
  474.6 24.9 %collective-permute-done = f32[32,64,128]{2,1,0:T(8,128)S(1)} collective-permute-done((f32[32,64,128]{2,1,0:T(8,128)S(1)}, f32[32,64,128]{2,1,0:T(8,128)S(1)}, u32[]{:S(2)}, u32[]{:S(2)}) %collective-permute-start) | collective-permute-done | bytes 1048608 | tf_op jit(solution)/shard_map/while/body/eval_jaxpr/ppermute | solution.py:15
  500.2 1.9 collective-permute-start
  502.1 23.9 %collective-permute-done = f32[32,64,128]{2,1,0:T(8,128)S(1)} collective-permute-done((f32[32,64,128]{2,1,0:T(8,128)S(1)}, f32[32,64,128]{2,1,0:T(8,128)S(1)}, u32[]{:S(2)}, u32[]{:S(2)}) %collective-permute-start) | collective-permute-done | bytes 1048608 | tf_op jit(solution)/shard_map/while/body/eval_jaxpr/ppermute | solution.py:15
  526.8 1.9 collective-permute-start
  528.8 23.0 %collective-permute-done = f32[32,64,128]{2,1,0:T(8,128)S(1)} collective-permute-done((f32[32,64,128]{2,1,0:T(8,128)S(1)}, f32[32,64,128]{2,1,0:T(8,128)S(1)}, u32[]{:S(2)}, u32[]{:S(2)}) %collective-permute-start) | collective-permute-done | bytes 1048608 | tf_op jit(solution)/shard_map/while/body/eval_jaxpr/ppermute | solution.py:15
  552.6 1.9 collective-permute-start
  554.5 22.1 %collective-permute-done = f32[32,64,128]{2,1,0:T(8,128)S(1)} collective-permute-done((f32[32,64,128]{2,1,0:T(8,128)S(1)}, f32[32,64,128]{2,1,0:T(8,128)S(1)}, u32[]{:S(2)}, u32[]{:S(2)}) %collective-permute-start) | collective-permute-done | bytes 1048608 | tf_op jit(solution)/shard_map/while/body/eval_jaxpr/ppermute | solution.py:15
  577.3 1.9 collective-permute-start
  579.3 21.2 %collective-permute-done = f32[32,64,128]{2,1,0:T(8,128)S(1)} collective-permute-done((f32[32,64,128]{2,1,0:T(8,128)S(1)}, f32[32,64,128]{2,1,0:T(8,128)S(1)}, u32[]{:S(2)}, u32[]{:S(2)}) %collective-permute-start) | collective-permute-done | bytes 1048608 | tf_op jit(solution)/shard_map/while/body/eval_jaxpr/ppermute | solution.py:15
  601.2 1.9 collective-permute-start
  603.1 20.6 %collective-permute-done = f32[32,64,128]{2,1,0:T(8,128)S(1)} collective-permute-done((f32[32,64,128]{2,1,0:T(8,128)S(1)}, f32[32,64,128]{2,1,0:T(8,128)S(1)}, u32[]{:S(2)}, u32[]{:S(2)}) %collective-permute-start) | collective-permute-done | bytes 1048608 | tf_op jit(solution)/shard_map/while/body/eval_jaxpr/ppermute | solution.py:15
  624.5 1.9 collective-permute-start
  626.5 20.6 %collective-permute-done = f32[32,64,128]{2,1,0:T(8,128)S(1)} collective-permute-done((f32[32,64,128]{2,1,0:T(8,128)S(1)}, f32[32,64,128]{2,1,0:T(8,128)S(1)}, u32[]{:S(2)}, u32[]{:S(2)}) %collective-permute-start) | collective-permute-done | bytes 1048608 | tf_op jit(solution)/shard_map/while/body/eval_jaxpr/ppermute | solution.py:15
  647.9 1.9 collective-permute-start
  649.8 20.6 %collective-permute-done = f32[32,64,128]{2,1,0:T(8,128)S(1)} collective-permute-done((f32[32,64,128]{2,1,0:T(8,128)S(1)}, f32[32,64,128]{2,1,0:T(8,128)S(1)}, u32[]{:S(2)}, u32[]{:S(2)}) %collective-permute-start) | collective-permute-done | bytes 1048608 | tf_op jit(solution)/shard_map/while/body/eval_jaxpr/ppermute | solution.py:15
  671.2 1.9 collective-permute-start
  673.1 20.6 %collective-permute-done = f32[32,64,128]{2,1,0:T(8,128)S(1)} collective-permute-done((f32[32,64,128]{2,1,0:T(8,128)S(1)}, f32[32,64,128]{2,1,0:T(8,128)S(1)}, u32[]{:S(2)}, u32[]{:S(2)}) %collective-permute-start) | collective-permute-done | bytes 1048608 | tf_op jit(solution)/shard_map/while/body/eval_jaxpr/ppermute | solution.py:15
  696.5 20.9 %collective-permute-done = f32[32,64,128]{2,1,0:T(8,128)S(1)} collective-permute-done((f32[32,64,128]{2,1,0:T(8,128)S(1)}, f32[32,64,128]{2,1,0:T(8,128)S(1)}, u32[]{:S(2)}, u32[]{:S(2)}) %collective-permute-start) | collective-permute-done | bytes 1048608 | tf_op jit(solution)/shard_map/while/body/eval_jaxpr/ppermute | solution.py:15
  720.0 22.0 %collective-permute-done = f32[32,64,128]{2,1,0:T(8,128)S(1)} collective-permute-done((f32[32,64,128]{2,1,0:T(8,128)S(1)}, f32[32,64,128]{2,1,0:T(8,128)S(1)}, u32[]{:S(2)}, u32[]{:S(2)}) %collective-permute-start) | collective-permute-done | bytes 1048608 | tf_op jit(solution)/shard_map/while/body/eval_jaxpr/ppermute | solution.py:15
  742.8 1.9 collective-permute-start
  744.7 23.1 %collective-permute-done = f32[32,64,128]{2,1,0:T(8,128)S(1)} collective-permute-done((f32[32,64,128]{2,1,0:T(8,128)S(1)}, f32[32,64,128]{2,1,0:T(8,128)S(1)}, u32[]{:S(2)}, u32[]{:S(2)}) %collective-permute-start) | collective-permute-done | bytes 1048608 | tf_op jit(solution)/shard_map/while/body/eval_jaxpr/ppermute | solution.py:15
  770.5 16.9 %collective-permute-done = f32[32,64,128]{2,1,0:T(8,128)S(1)} collective-permute-done((f32[32,64,128]{2,1,0:T(8,128)S(1)}, f32[32,64,128]{2,1,0:T(8,128)S(1)}, u32[]{:S(2)}, u32[]{:S(2)}) %collective-permute-start) | collective-permute-done | bytes 1048608 | tf_op jit(solution)/shard_map/while/body/eval_jaxpr/ppermute | solution.py:15
  787.4 5.6 bitcast_multiply_fusion
  792.9 9.6 %multiply_reduce_fusion = (f32[1024]{0:T(1024)S(1)}, f32[1024,2048]{0,1:T(8,128)S(1)}) fusion(bf16[1024,2048]{0,1:T(8,128)(2,1)} %copy.71, f32[1024,2048]{0,1:T(8,128)S(1)} %copy-done.1, f32[2048]{0:T(1024)S(1)} %copy-done.6, f32[1024,1,32,64]{0,3,2,1:T(8,128)} %bitcast_multiply_fusion, f32[256,8,8,128]{3,2,1,0:T(8,128)} %bitcast.145), kind=kLoop, calls=%fused_computation.66 | loop fusion | flops 23067648 | bytes 37761024 | tf_op jit(solution)/shard_map/reduce_sum | solution.py:82
  802.6 2.4 multiply_convert_fusion
  804.9 6.4 copy.72
  (187 shorter events, 82.3 us)
Async XLA Ops:
  1.1 38.6 %collective-permute-start.1 = (bf16[3,2048]{0,1:T(8,128)(2,1)S(1)}, bf16[3,2048]{0,1:T(8,128)(2,1)S(1)}, u32[]{:S(2)}, u32[]{:S(2)}) collective-permute-start(bf16[3,2048]{0,1:T(8,128)(2,1)S(1)} %copy.65), channel_id=1, source_target_pairs={{0,8},{8,16},{16,24},{24,32},{32,40},{40,48},{48,56},{56,64},{64,7... | collective-permute-start | bytes 36872 | tf_op jit(solution)/shard_map/ppermute | solution.py:15
  24.1 6.5 copy-start.4
  24.1 7.5 copy-start.5
  24.1 14.9 %copy-start.8 = (f32[32]{0:T(128)S(1)}, f32[32]{0:T(128)}, u32[]{:S(2)}) copy-start(f32[32]{0:T(128)} %param.20) | copy-start | bytes 388
  58.5 5.7 copy-start
  58.5 5.7 copy-start.2
  413.9 373.5 %copy-start.3 = (f32[1024,32]{0,1:T(8,128)S(1)}, f32[1024,32]{0,1:T(8,128)}, u32[]{:S(2)}) copy-start(f32[1024,32]{0,1:T(8,128)} %fusion.50) | copy-start | bytes 393220
  414.8 28.6 %collective-permute-start = (f32[32,64,128]{2,1,0:T(8,128)S(1)}, f32[32,64,128]{2,1,0:T(8,128)S(1)}, u32[]{:S(2)}, u32[]{:S(2)}) collective-permute-start(f32[32,64,128]{2,1,0:T(8,128)S(1)} %multiply_add_fusion.2), channel_id=1, source_target_pairs={{0,8},{8,16},{16,24},{24,32},{32,40},{40,48},{48,56},{56,64},{64,7... | collective-permute-start | bytes 3145736 | tf_op jit(solution)/shard_map/while/body/eval_jaxpr/ppermute | solution.py:15
  444.2 27.7 %collective-permute-start = (f32[32,64,128]{2,1,0:T(8,128)S(1)}, f32[32,64,128]{2,1,0:T(8,128)S(1)}, u32[]{:S(2)}, u32[]{:S(2)}) collective-permute-start(f32[32,64,128]{2,1,0:T(8,128)S(1)} %multiply_add_fusion.2), channel_id=1, source_target_pairs={{0,8},{8,16},{16,24},{24,32},{32,40},{40,48},{48,56},{56,64},{64,7... | collective-permute-start | bytes 3145736 | tf_op jit(solution)/shard_map/while/body/eval_jaxpr/ppermute | solution.py:15
  472.7 26.8 %collective-permute-start = (f32[32,64,128]{2,1,0:T(8,128)S(1)}, f32[32,64,128]{2,1,0:T(8,128)S(1)}, u32[]{:S(2)}, u32[]{:S(2)}) collective-permute-start(f32[32,64,128]{2,1,0:T(8,128)S(1)} %multiply_add_fusion.2), channel_id=1, source_target_pairs={{0,8},{8,16},{16,24},{24,32},{32,40},{40,48},{48,56},{56,64},{64,7... | collective-permute-start | bytes 3145736 | tf_op jit(solution)/shard_map/while/body/eval_jaxpr/ppermute | solution.py:15
  500.2 25.9 %collective-permute-start = (f32[32,64,128]{2,1,0:T(8,128)S(1)}, f32[32,64,128]{2,1,0:T(8,128)S(1)}, u32[]{:S(2)}, u32[]{:S(2)}) collective-permute-start(f32[32,64,128]{2,1,0:T(8,128)S(1)} %multiply_add_fusion.2), channel_id=1, source_target_pairs={{0,8},{8,16},{16,24},{24,32},{32,40},{40,48},{48,56},{56,64},{64,7... | collective-permute-start | bytes 3145736 | tf_op jit(solution)/shard_map/while/body/eval_jaxpr/ppermute | solution.py:15
  526.8 24.9 %collective-permute-start = (f32[32,64,128]{2,1,0:T(8,128)S(1)}, f32[32,64,128]{2,1,0:T(8,128)S(1)}, u32[]{:S(2)}, u32[]{:S(2)}) collective-permute-start(f32[32,64,128]{2,1,0:T(8,128)S(1)} %multiply_add_fusion.2), channel_id=1, source_target_pairs={{0,8},{8,16},{16,24},{24,32},{32,40},{40,48},{48,56},{56,64},{64,7... | collective-permute-start | bytes 3145736 | tf_op jit(solution)/shard_map/while/body/eval_jaxpr/ppermute | solution.py:15
  552.6 24.0 %collective-permute-start = (f32[32,64,128]{2,1,0:T(8,128)S(1)}, f32[32,64,128]{2,1,0:T(8,128)S(1)}, u32[]{:S(2)}, u32[]{:S(2)}) collective-permute-start(f32[32,64,128]{2,1,0:T(8,128)S(1)} %multiply_add_fusion.2), channel_id=1, source_target_pairs={{0,8},{8,16},{16,24},{24,32},{32,40},{40,48},{48,56},{56,64},{64,7... | collective-permute-start | bytes 3145736 | tf_op jit(solution)/shard_map/while/body/eval_jaxpr/ppermute | solution.py:15
  577.3 23.1 %collective-permute-start = (f32[32,64,128]{2,1,0:T(8,128)S(1)}, f32[32,64,128]{2,1,0:T(8,128)S(1)}, u32[]{:S(2)}, u32[]{:S(2)}) collective-permute-start(f32[32,64,128]{2,1,0:T(8,128)S(1)} %multiply_add_fusion.2), channel_id=1, source_target_pairs={{0,8},{8,16},{16,24},{24,32},{32,40},{40,48},{48,56},{56,64},{64,7... | collective-permute-start | bytes 3145736 | tf_op jit(solution)/shard_map/while/body/eval_jaxpr/ppermute | solution.py:15
  601.2 22.6 %collective-permute-start = (f32[32,64,128]{2,1,0:T(8,128)S(1)}, f32[32,64,128]{2,1,0:T(8,128)S(1)}, u32[]{:S(2)}, u32[]{:S(2)}) collective-permute-start(f32[32,64,128]{2,1,0:T(8,128)S(1)} %multiply_add_fusion.2), channel_id=1, source_target_pairs={{0,8},{8,16},{16,24},{24,32},{32,40},{40,48},{48,56},{56,64},{64,7... | collective-permute-start | bytes 3145736 | tf_op jit(solution)/shard_map/while/body/eval_jaxpr/ppermute | solution.py:15
  624.5 22.6 %collective-permute-start = (f32[32,64,128]{2,1,0:T(8,128)S(1)}, f32[32,64,128]{2,1,0:T(8,128)S(1)}, u32[]{:S(2)}, u32[]{:S(2)}) collective-permute-start(f32[32,64,128]{2,1,0:T(8,128)S(1)} %multiply_add_fusion.2), channel_id=1, source_target_pairs={{0,8},{8,16},{16,24},{24,32},{32,40},{40,48},{48,56},{56,64},{64,7... | collective-permute-start | bytes 3145736 | tf_op jit(solution)/shard_map/while/body/eval_jaxpr/ppermute | solution.py:15
  647.9 22.6 %collective-permute-start = (f32[32,64,128]{2,1,0:T(8,128)S(1)}, f32[32,64,128]{2,1,0:T(8,128)S(1)}, u32[]{:S(2)}, u32[]{:S(2)}) collective-permute-start(f32[32,64,128]{2,1,0:T(8,128)S(1)} %multiply_add_fusion.2), channel_id=1, source_target_pairs={{0,8},{8,16},{16,24},{24,32},{32,40},{40,48},{48,56},{56,64},{64,7... | collective-permute-start | bytes 3145736 | tf_op jit(solution)/shard_map/while/body/eval_jaxpr/ppermute | solution.py:15
  671.2 22.6 %collective-permute-start = (f32[32,64,128]{2,1,0:T(8,128)S(1)}, f32[32,64,128]{2,1,0:T(8,128)S(1)}, u32[]{:S(2)}, u32[]{:S(2)}) collective-permute-start(f32[32,64,128]{2,1,0:T(8,128)S(1)} %multiply_add_fusion.2), channel_id=1, source_target_pairs={{0,8},{8,16},{16,24},{24,32},{32,40},{40,48},{48,56},{56,64},{64,7... | collective-permute-start | bytes 3145736 | tf_op jit(solution)/shard_map/while/body/eval_jaxpr/ppermute | solution.py:15
  694.5 22.8 %collective-permute-start = (f32[32,64,128]{2,1,0:T(8,128)S(1)}, f32[32,64,128]{2,1,0:T(8,128)S(1)}, u32[]{:S(2)}, u32[]{:S(2)}) collective-permute-start(f32[32,64,128]{2,1,0:T(8,128)S(1)} %multiply_add_fusion.2), channel_id=1, source_target_pairs={{0,8},{8,16},{16,24},{24,32},{32,40},{40,48},{48,56},{56,64},{64,7... | collective-permute-start | bytes 3145736 | tf_op jit(solution)/shard_map/while/body/eval_jaxpr/ppermute | solution.py:15
  718.1 23.9 %collective-permute-start = (f32[32,64,128]{2,1,0:T(8,128)S(1)}, f32[32,64,128]{2,1,0:T(8,128)S(1)}, u32[]{:S(2)}, u32[]{:S(2)}) collective-permute-start(f32[32,64,128]{2,1,0:T(8,128)S(1)} %multiply_add_fusion.2), channel_id=1, source_target_pairs={{0,8},{8,16},{16,24},{24,32},{32,40},{40,48},{48,56},{56,64},{64,7... | collective-permute-start | bytes 3145736 | tf_op jit(solution)/shard_map/while/body/eval_jaxpr/ppermute | solution.py:15
  742.8 25.0 %collective-permute-start = (f32[32,64,128]{2,1,0:T(8,128)S(1)}, f32[32,64,128]{2,1,0:T(8,128)S(1)}, u32[]{:S(2)}, u32[]{:S(2)}) collective-permute-start(f32[32,64,128]{2,1,0:T(8,128)S(1)} %multiply_add_fusion.2), channel_id=1, source_target_pairs={{0,8},{8,16},{16,24},{24,32},{32,40},{40,48},{48,56},{56,64},{64,7... | collective-permute-start | bytes 3145736 | tf_op jit(solution)/shard_map/while/body/eval_jaxpr/ppermute | solution.py:15
  768.5 18.8 %collective-permute-start = (f32[32,64,128]{2,1,0:T(8,128)S(1)}, f32[32,64,128]{2,1,0:T(8,128)S(1)}, u32[]{:S(2)}, u32[]{:S(2)}) collective-permute-start(f32[32,64,128]{2,1,0:T(8,128)S(1)} %multiply_add_fusion.2), channel_id=1, source_target_pairs={{0,8},{8,16},{16,24},{24,32},{32,40},{40,48},{48,56},{56,64},{64,7... | collective-permute-start | bytes 3145736 | tf_op jit(solution)/shard_map/while/body/eval_jaxpr/ppermute | solution.py:15
  787.3 5.6 copy-start.1
  787.4 5.6 copy-start.6
  792.9 9.6 %copy-start.7 = (f32[2048]{0:T(1024)S(1)}, f32[2048]{0:T(1024)}, u32[]{:S(2)}) copy-start(f32[2048]{0:T(1024)} %param.21) | copy-start | bytes 24580
where the time goes:
time: 820 us; the launch traced here: 811 us
  waiting for transfers between devices  331 us (40%)
  local copies, waits for them, and re-layouts  292 us (36%)
  matrix products  85.7 us (10%)
  other arithmetic  67 us (8%)
  starting transfers between devices  34.5 us (4%)
    ppermute x16, waiting for transfers between devices, shifted(): lax.ppermute(value, axis, [(source, source + steps) for source in range(i...  331 us
    dynamic_update_slice x8, local copies, waits for them, and re-layouts, run_spans(): lax.scan(span_step, initial, (fold_rows(input_rows), fold_rows(step_rows)...  218 us
    dot_general x8, matrix products, span_step(): jnp.einsum('tsgh,sghp->tghp', mixing, input_grp, precision=lax.Precision....  42.4 us
    ppermute x16, starting transfers between devices, shifted(): lax.ppermute(value, axis, [(source, source + steps) for source in range(i...  34.5 us
    dynamic_slice x8, local copies, waits for them, and re-layouts, run_spans(): lax.scan(span_step, initial, (fold_rows(input_rows), fold_rows(step_rows)...  30.9 us
    unnamed x23, local copies, waits for them, and re-layouts  19.5 us
    mul x1, other arithmetic, shards(): conv_in = jax.nn.silu(total)  18.7 us
  transfers between devices with their start and end apart: 16, of which 15 were waited for; matrix products, arithmetic and copies ran while one was open for 4% of the time, Pallas kernels for 0%

commit v1 on v0

v1 whole, which is shorter than its diff:
```python
import functools

import jax
import jax.numpy as jnp
from jax import lax
from jax.experimental import pallas as pl
from jax.experimental.pallas import tpu as pltpu
from jax.sharding import PartitionSpec as P

F32 = jnp.float32
BF16 = jnp.bfloat16
HEAD = 64
STATE = 128
TAPS = 4
CHUNK = 128
LANES = 256
EXTRA = 16
HIGHEST = lax.Precision.HIGHEST
VMEM_BYTES = 24 * 1024 * 1024


def iota(shape, dim):
    return lax.broadcasted_iota(jnp.int32, shape, dim)


def dot(a, b):
    return jnp.dot(a, b, preferred_element_type=F32)


def dot_exact(a, b):
    return jnp.dot(a, b, preferred_element_type=F32, precision=HIGHEST)


def split(value):
    high = value.astype(BF16)
    return high, (value - high.astype(F32)).astype(BF16)


def silu_of_half(half):
    return half * jnp.tanh(half) + half


def encode(value):
    top = jnp.max(jnp.abs(value), axis=0, keepdims=True)
    scale = jnp.maximum(top * 1.00390625, 1e-30).astype(BF16).astype(F32)
    size = jnp.exp2(jnp.abs(value) * (252.0 / scale) - 126.0)
    return jnp.where(value < 0, -size, size).astype(BF16), scale


def decode(code, scale):
    code = code.astype(F32)
    size = (jnp.log2(jnp.abs(code)) + 126.0) * (scale * (1.0 / 252.0))
    return jnp.where(code < 0, -size, size)


def stack_chunks(value):
    pieces = value.shape[1] // CHUNK
    return jnp.concatenate([value[:, CHUNK * c : CHUNK * (c + 1)] for c in range(pieces)], axis=0)


def head_spread(heads, channels):
    return (iota((heads, channels), 0) == iota((heads, channels), 1) // HEAD).astype(F32)


def store_tokens(ref, value, heads):
    for c in range(value.shape[0] // heads):
        part = value[heads * c : heads * (c + 1)]
        high = part.astype(BF16).astype(F32)
        both = jnp.concatenate([high, part - high], axis=0)
        ref[CHUNK * c : CHUNK * (c + 1), :] = both.T.astype(BF16)


def conv_half(rows, weight):
    weight = weight * 0.5
    back = pltpu.roll(rows, 1, 0)
    near = rows * weight[3:4] + back * weight[2:3]
    far = rows * weight[1:2] + back * weight[0:1]
    return (near + pltpu.roll(far, 2, 0))[16:]


def end_state_kernel(
    x_ref, weight_ref, write_ref, step_ref, decay_ref, out_ref, gains, spread, keys, parts, packed
):
    heads, tokens = step_ref.shape
    pieces = tokens // CHUNK
    channels = heads * HEAD
    turn = pl.program_id(0)

    @pl.when(turn == 0)
    def prepare():
        decay = decay_ref[...]
        logs = stack_chunks(decay)
        later = (iota((CHUNK, CHUNK), 0) > iota((CHUNK, CHUNK), 1)).astype(F32)
        suffix = dot_exact(logs, later)
        total = suffix[:, 0:1] + logs[:, 0:1]
        offset = jnp.zeros((heads, 1), F32)
        offsets = []
        for c in reversed(range(pieces)):
            offsets.append(offset)
            offset = offset + total[heads * c : heads * (c + 1)]
        suffix = suffix + jnp.concatenate(offsets[::-1], axis=0)
        gain = jnp.exp(suffix) * stack_chunks(step_ref[...])
        row, lane = (iota(gain.shape, 0), iota(gain.shape, 1))
        gain = jnp.where((row < heads) & (lane < TAPS - 1), 0.0, gain)
        store_tokens(gains, gain, heads)
        ones = head_spread(heads, channels)
        spread[...] = jnp.concatenate([ones, ones], axis=0).astype(BF16)
        write_t = write_ref[...].astype(F32).T.astype(BF16)
        keys[...] = jnp.concatenate([write_t, write_t], axis=1)
        first = decay[:, 0:CHUNK]
        lane = iota(first.shape, 1)
        run0 = first[:, 0:1]
        run1 = run0 + first[:, 1:2]
        run2 = run1 + first[:, 2:3]
        step = step_ref[:, 0:CHUNK]
        scalars = jnp.where(lane == 0, jnp.exp(offset), 0.0)
        for t, run in enumerate((run0, run1, run2)):
            scalars = jnp.where(lane == t + 1, jnp.exp(-run) * step[:, t : t + 1], scalars)
        wide = dot_exact(scalars.T[0:8], ones)
        segment = (iota(wide.shape, 1) % HEAD) // (HEAD // 4)
        packed[...] = jnp.broadcast_to(
            jnp.sum(jnp.where(iota(wide.shape, 0) == segment, wide, 0.0), axis=0, keepdims=True),
            packed.shape,
        )

    lanes = pl.ds(pl.multiple_of(turn * LANES, LANES), LANES)
    weight = weight_ref[...]
    for c in range(pieces):
        if c == 0:
            rows = jnp.concatenate([jnp.zeros((16, LANES), BF16), x_ref[0:CHUNK]], axis=0)
        else:
            rows = x_ref[CHUNK * c - 16 : CHUNK * (c + 1)]
        value = silu_of_half(conv_half(rows.astype(F32), weight))
        gain = dot(gains[CHUNK * c : CHUNK * (c + 1)], spread[:, lanes])
        high, low = split(value * gain)
        parts[CHUNK * c : CHUNK * (c + 1)] = high
        parts[tokens + CHUNK * c : tokens + CHUNK * (c + 1)] = low
    state = dot(keys[...], parts[...])
    code, scale = encode(state)
    row = iota((EXTRA, LANES), 0)
    first = pltpu.roll(x_ref[0:16].astype(F32), 7, 0)
    last = pltpu.roll(x_ref[tokens - 16 : tokens].astype(F32), 7, 0)
    writes = pltpu.roll(write_ref[0:16].astype(F32), 1, 0)
    writes = jnp.concatenate([writes] * (LANES // STATE), axis=1)
    scalar = packed[0:1, lanes]
    high = scalar.astype(BF16).astype(F32)
    middle = (scalar - high).astype(BF16).astype(F32)
    low = scalar - high - middle
    extra = jnp.where(row == 0, scale, 0.0)
    extra = jnp.where((row >= 1) & (row <= 3), writes, extra)
    extra = jnp.where((row >= 4) & (row <= 6), last, extra)
    extra = jnp.where((row >= 7) & (row <= 9), first, extra)
    extra = jnp.where(row == 10, high, extra)
    extra = jnp.where(row == 11, middle, extra)
    extra = jnp.where(row == 12, low, extra).astype(BF16)
    for part in range(LANES // 128):
        out_ref[part, 0:STATE] = code[:, 128 * part : 128 * (part + 1)]
        out_ref[part, STATE : STATE + EXTRA] = extra[:, 128 * part : 128 * (part + 1)]


def end_state(x, weight, write, step, decay):
    tokens, channels = x.shape
    heads = step.shape[0]
    owners = channels // 128
    return pl.pallas_call(
        end_state_kernel,
        grid=(channels // LANES,),
        in_specs=[
            pl.BlockSpec((tokens, LANES), lambda j: (0, j)),
            pl.BlockSpec((TAPS, LANES), lambda j: (0, j)),
            pl.BlockSpec((tokens, STATE), lambda j: (0, 0)),
            pl.BlockSpec((heads, tokens), lambda j: (0, 0)),
            pl.BlockSpec((heads, tokens), lambda j: (0, 0)),
        ],
        out_specs=pl.BlockSpec((LANES // 128, STATE + EXTRA, 128), lambda j: (j, 0, 0)),
        out_shape=jax.ShapeDtypeStruct((owners, STATE + EXTRA, 128), BF16),
        scratch_shapes=[
            pltpu.VMEM((tokens, 2 * heads), BF16),
            pltpu.VMEM((2 * heads, channels), BF16),
            pltpu.VMEM((STATE, 2 * tokens), BF16),
            pltpu.VMEM((2 * tokens, LANES), BF16),
            pltpu.VMEM((8, channels), F32),
        ],
        compiler_params=pltpu.CompilerParams(vmem_limit_bytes=VMEM_BYTES),
        name="end_state",
    )(x, weight, write, step, decay)


def prefix_kernel(in_ref, weight_ref, out_ref, blocks):
    count = in_ref.shape[0]
    tile = in_ref[:, STATE : STATE + EXTRA, :].astype(F32)
    shape = tile.shape
    row, lane = (iota(shape, 1), iota(shape, 2))
    before = jnp.concatenate([jnp.zeros((1,) + shape[1:], F32), tile[:-1]], axis=0)
    rows = jnp.where(
        (row >= 4) & (row <= 6), before, jnp.where((row >= 7) & (row <= 9), tile, 0.0)
    )
    weight = weight_ref[...] * 0.5
    half = rows * weight[3:4][None]
    for back in range(1, TAPS):
        half = half + pltpu.roll(rows, back, 1) * weight[3 - back : 4 - back][None]
    value = silu_of_half(half)
    scalars = jnp.sum(jnp.where((row >= 10) & (row <= 12), tile, 0.0), axis=1, keepdims=True)
    left = iota(scalars.shape, 2) < HEAD

    def spread_of(segment):
        place = segment * (HEAD // 4)
        return jnp.where(
            left, scalars[:, :, place : place + 1], scalars[:, :, HEAD + place : HEAD + place + 1]
        )

    fade = spread_of(0)
    gain = jnp.where(row == 7, spread_of(1), jnp.where(row == 8, spread_of(2), spread_of(3)))
    value = jnp.where((row >= 7) & (row <= 9), value * gain, 0.0)
    value = pltpu.roll(value, EXTRA - 6, 1)
    high = value.astype(BF16)
    low = (value - high.astype(F32)).astype(BF16)
    keys = jnp.where((row >= 1) & (row <= 3), tile, 0.0).reshape(count * EXTRA, 128).T.astype(BF16)
    blocks[...] = jnp.zeros(blocks.shape, BF16)
    for j in range(count):
        blocks[EXTRA * j : EXTRA * (j + 1), 128 * j : 128 * (j + 1)] = high[j]
        blocks[EXTRA * (count + j) : EXTRA * (count + j + 1), 128 * j : 128 * (j + 1)] = low[j]
    first = dot(jnp.concatenate([keys, keys], axis=1), blocks[...])
    state = jnp.zeros((STATE, 128), F32)
    zero_rows = jnp.zeros((EXTRA, 128), F32)
    for j in range(count):
        code, scale = encode(state)
        out_ref[j, 0:STATE] = code
        out_ref[j, STATE : STATE + EXTRA] = (zero_rows + scale).astype(BF16)
        local = decode(in_ref[j, 0:STATE], tile[j, 0:1])
        state = fade[j] * (state + first[:, 128 * j : 128 * (j + 1)]) + local


def prefix(received, weight):
    count = received.shape[0]
    whole = pl.BlockSpec(memory_space=pltpu.VMEM)
    return pl.pallas_call(
        prefix_kernel,
        in_specs=[whole, whole],
        out_specs=whole,
        out_shape=jax.ShapeDtypeStruct(received.shape, BF16),
        scratch_shapes=[pltpu.VMEM((2 * count * EXTRA, count * 128), BF16)],
        compiler_params=pltpu.CompilerParams(vmem_limit_bytes=VMEM_BYTES),
        name="prefix",
    )(received, weight)


def local_kernel(
    x_ref,
    halo_ref,
    weight_ref,
    gate_ref,
    write_ref,
    read_ref,
    step_ref,
    decay_ref,
    skip_ref,
    own_ref,
    reach_ref,
    gains,
    fades,
    spread,
    keys,
    mix_a,
    mix_b,
    rowed,
    parts,
):
    heads, tokens = step_ref.shape
    pieces = tokens // CHUNK
    channels = heads * HEAD
    turn = pl.program_id(0)

    @pl.when(turn == 0)
    def prepare():
        logs = stack_chunks(decay_ref[...])
        upto = (iota((CHUNK, CHUNK), 0) <= iota((CHUNK, CHUNK), 1)).astype(F32)
        run = dot_exact(logs, upto)
        middle = run[:, CHUNK // 2 - 1 : CHUNK // 2]
        total = run[:, CHUNK - 1 : CHUNK]
        store_tokens(gains, jnp.exp(middle - run) * stack_chunks(step_ref[...]), heads)
        store_tokens(fades, jnp.exp(run - middle), heads)
        ones = head_spread(heads, channels)
        spread[...] = jnp.concatenate([ones, ones], axis=0).astype(BF16)
        lane = iota((heads, 128), 1)
        scalars = jnp.where(lane == 2 * pieces, skip_ref[...], 0.0)
        offset = jnp.zeros((heads, 1), F32)
        for c in range(pieces):
            mid = middle[heads * c : heads * (c + 1)]
            tot = total[heads * c : heads * (c + 1)]
            scalars = jnp.where(lane == c, jnp.exp(offset + mid), scalars)
            offset = offset + tot
            if c + 1 < pieces:
                onward = jnp.exp(middle[heads * (c + 1) : heads * (c + 2)] + (tot - mid))
                scalars = jnp.where(lane == pieces + c, onward, scalars)
        rowed[...] = dot_exact(scalars.T[0 : rowed.shape[0]], ones)
        causal = iota((CHUNK, CHUNK), 0) >= iota((CHUNK, CHUNK), 1)
        for c in range(pieces):
            span = slice(CHUNK * c, CHUNK * (c + 1))
            write = write_ref[span]
            read = read_ref[span]
            mixing = lax.dot_general(
                read, write, (((1,), (1,)), ((), ())), preferred_element_type=F32
            )
            high, low = split(jnp.where(causal, mixing, 0.0))
            mix_a[span] = jnp.concatenate([high, high], axis=1)
            mix_b[span] = jnp.concatenate([low, read], axis=1)
            write_t = write.astype(F32).T.astype(BF16)
            keys[span] = jnp.concatenate([write_t, write_t], axis=1)

    lanes = pl.ds(pl.multiple_of(turn * LANES, LANES), LANES)
    weight = weight_ref[...]
    skip = rowed[2 * pieces : 2 * pieces + 1, lanes]
    state = jnp.zeros((STATE, LANES), F32)
    for c in range(pieces):
        span = slice(CHUNK * c, CHUNK * (c + 1))
        if c == 0:
            rows = jnp.concatenate([halo_ref[...], x_ref[0:CHUNK]], axis=0)
        else:
            rows = x_ref[CHUNK * c - 16 : CHUNK * (c + 1)]
        value = silu_of_half(conv_half(rows.astype(F32), weight))
        gain = dot(gains[span], spread[:, lanes])
        high, low = split(value * gain)
        parts[0:CHUNK] = high
        parts[CHUNK : 2 * CHUNK] = low
        both = parts[0 : 2 * CHUNK]
        mixed = dot(mix_a[span], both)
        if c == 0:
            mixed = mixed + dot(mix_b[span, 0:CHUNK], high)
        else:
            state_high, state_low = split(state)
            mixed = mixed + dot(mix_b[span], jnp.concatenate([high, state_high], axis=0))
            mixed = mixed + dot(mix_b[span, CHUNK : 2 * CHUNK], state_low)
        if c + 1 < pieces:
            onward = rowed[pieces + c : pieces + c + 1, lanes]
            state = onward * (state + dot(keys[span], both))
        fade = dot(fades[span], spread[:, lanes])
        opened = silu_of_half(gate_ref[span].astype(F32) * 0.5)
        own_ref[span, lanes] = (mixed * fade + skip * value) * opened
        reach_ref[span, lanes] = fade * opened * rowed[c : c + 1, lanes]


def local_part(x, halo, weight, gate, write, read, step, decay, skip):
    tokens, channels = x.shape
    heads = step.shape[0]
    pieces = tokens // CHUNK
    return pl.pallas_call(
        local_kernel,
        grid=(channels // LANES,),
        in_specs=[
            pl.BlockSpec((tokens, LANES), lambda j: (0, j)),
            pl.BlockSpec((16, LANES), lambda j: (0, j)),
            pl.BlockSpec((TAPS, LANES), lambda j: (0, j)),
            pl.BlockSpec((tokens, LANES), lambda j: (0, j)),
            pl.BlockSpec((tokens, STATE), lambda j: (0, 0)),
            pl.BlockSpec((tokens, STATE), lambda j: (0, 0)),
            pl.BlockSpec((heads, tokens), lambda j: (0, 0)),
            pl.BlockSpec((heads, tokens), lambda j: (0, 0)),
            pl.BlockSpec((heads, 1), lambda j: (0, 0)),
        ],
        out_specs=[pl.BlockSpec(memory_space=pltpu.VMEM)] * 2,
        out_shape=[pltpu.VMEM((tokens, channels), F32)] * 2,
        scratch_shapes=[
            pltpu.VMEM((tokens, 2 * heads), BF16),
            pltpu.VMEM((tokens, 2 * heads), BF16),
            pltpu.VMEM((2 * heads, channels), BF16),
            pltpu.VMEM((tokens, 2 * CHUNK), BF16),
            pltpu.VMEM((tokens, 2 * CHUNK), BF16),
            pltpu.VMEM((tokens, 2 * CHUNK), BF16),
            pltpu.VMEM((2 * pieces + 8, channels), F32),
            pltpu.VMEM((2 * CHUNK, LANES), BF16),
        ],
        compiler_params=pltpu.CompilerParams(vmem_limit_bytes=VMEM_BYTES),
        name="local_part",
    )(x, halo, weight, gate, write, read, step, decay, skip)


def final_kernel(state_ref, read_ref, own_ref, reach_ref, gain_ref, out_ref, states, gated):
    owners = state_ref.shape[0]
    turn = pl.program_id(0)
    rows = out_ref.shape[0]
    channels = owners * 128

    @pl.when(turn == 0)
    def prepare():
        for k in range(owners):
            value = decode(state_ref[k, 0:STATE], state_ref[k, STATE : STATE + 1].astype(F32))
            high, low = split(value)
            states[0:STATE, 128 * k : 128 * (k + 1)] = high
            states[STATE : 2 * STATE, 128 * k : 128 * (k + 1)] = low

    read = read_ref[...]
    both = jnp.concatenate([read, read], axis=1)
    start = pl.multiple_of(turn * rows, rows)
    squares = jnp.zeros((rows, 128), F32)
    for j in range(channels // LANES):
        lanes = slice(LANES * j, LANES * (j + 1))
        part = dot(both, states[:, lanes])
        part = own_ref[pl.ds(start, rows), lanes] + reach_ref[pl.ds(start, rows), lanes] * part
        gated[:, lanes] = part
        for i in range(LANES // 128):
            piece = part[:, 128 * i : 128 * (i + 1)]
            squares = squares + piece * piece
    inverse = lax.rsqrt(jnp.sum(squares, axis=1, keepdims=True) * (1.0 / channels) + 1e-05)
    for j in range(channels // LANES):
        lanes = slice(LANES * j, LANES * (j + 1))
        out_ref[:, lanes] = (gated[:, lanes] * inverse * gain_ref[:, lanes]).astype(BF16)


def final_part(entering, read, own, reach, norm_gain):
    tokens, channels = own.shape
    rows = 128
    whole = pl.BlockSpec(memory_space=pltpu.VMEM)
    return pl.pallas_call(
        final_kernel,
        grid=(tokens // rows,),
        in_specs=[
            whole,
            pl.BlockSpec((rows, STATE), lambda i: (i, 0)),
            whole,
            whole,
            pl.BlockSpec((1, channels), lambda i: (0, 0)),
        ],
        out_specs=pl.BlockSpec((rows, channels), lambda i: (i, 0)),
        out_shape=jax.ShapeDtypeStruct((tokens, channels), BF16),
        scratch_shapes=[
            pltpu.VMEM((2 * STATE, channels), BF16),
            pltpu.VMEM((rows, channels), F32),
        ],
        compiler_params=pltpu.CompilerParams(vmem_limit_bytes=VMEM_BYTES),
        name="final_part",
    )(entering, read, own, reach, norm_gain)


def shards(x, weight, gate, write, read, step, decay, skip, norm_gain):
    tokens, channels = x.shape
    count = lax.axis_size("ctx")
    place = lax.axis_index("ctx")
    ends = end_state(x, weight, write, step, decay)
    received = lax.all_to_all(ends, "ctx", 0, 0)
    last, ends = lax.optimization_barrier((x[tokens - 16 :], ends))
    halo = lax.ppermute(last, "ctx", [(i, i + 1) for i in range(count - 1)])
    owned = lax.dynamic_slice(weight, (0, place * 128), (TAPS, 128))
    entering = prefix(received, owned)
    halo, entering = lax.optimization_barrier((halo, entering))
    entering = lax.all_to_all(entering, "ctx", 0, 0)
    own, reach = local_part(x, halo, weight, gate, write, read, step, decay, skip[:, None])
    return final_part(entering, read, own, reach, norm_gain[None, :])


def solution(mesh):
    placed = (
        P("ctx", "tp"),
        P(None, "tp"),
        P("ctx", "tp"),
        P("ctx", "tp"),
        P("ctx", "tp"),
        P("tp", "ctx"),
        P("tp", "ctx"),
        P("tp"),
        P("tp"),
    )
    return jax.shard_map(
        shards, mesh=mesh, in_specs=placed, out_specs=P("ctx", "tp"), check_vma=False
    )
```

time: 820 us -> 88.5 us (0.11)
  the two profiles are of different devices: /device:TPU:22 before, /device:TPU:0 now
where the time goes in v1:
time: 88.5 us; the launch traced here: 87.5 us
  Pallas kernels  39.9 us (45%)
  local copies, waits for them, and re-layouts  24.3 us (27%)
  starting transfers between devices  15.8 us (18%)
  waiting for transfers between devices  7.43 us (8%)
    unnamed x36, local copies, waits for them, and re-layouts  23.3 us
    pallas_call x1, Pallas kernels, local_part(): pl.pallas_call(local_kernel, grid=(channels // LANES,), in_specs=[pl.Bloc...  21.4 us
    pallas_call x1, Pallas kernels, end_state(): pl.pallas_call(end_state_kernel, grid=(channels // LANES,), in_specs=[pl....  10.7 us
    all_to_all x1, starting transfers between devices, shards(): received = lax.all_to_all(ends, 'ctx', 0, 0)  8.13 us
    all_to_all x1, waiting for transfers between devices, shards(): received = lax.all_to_all(ends, 'ctx', 0, 0)  7.42 us
    pallas_call x1, Pallas kernels, final_part(): pl.pallas_call(final_kernel, grid=(tokens // rows,), in_specs=[whole, pl....  6.01 us
    all_to_all x1, starting transfers between devices, shards(): entering = lax.all_to_all(entering, 'ctx', 0, 0)  3.86 us
    ppermute x1, starting transfers between devices, shards(): halo = lax.ppermute(last, 'ctx', [(i, i + 1) for i in range(count - 1)])  3.82 us
  transfers between devices with their start and end apart: 3, of which 1 were waited for; matrix products, arithmetic and copies ran while one was open for 1% of the time, Pallas kernels for 27%

profile of v1, /device:TPU:0, one launch (start us, length us, event | category | flops | bytes accessed | tf_op | source)
XLA Modules:
  0.0 87.5 jit_solution(5714102351828556524)
XLA Ops:
  0.0 0.0 copy-start
  0.0 2.2 %copy-done = bf16[1024,2048]{1,0:T(8,128)(2,1)S(1)} copy-done((bf16[1024,2048]{1,0:T(8,128)(2,1)S(1)}, bf16[1024,2048]{1,0:T(8,128)(2,1)}, u32[]{:S(2)}) %copy-start) | copy-done | bytes 4194328
  2.2 0.0 copy-start.8
  2.2 0.9 %copy-done.8 = bf16[1024,128]{1,0:T(8,128)(2,1)S(1)} copy-done((bf16[1024,128]{1,0:T(8,128)(2,1)S(1)}, bf16[1024,128]{1,0:T(8,128)(2,1)}, u32[]{:S(2)}) %copy-start.8) | copy-done | bytes 262168
  3.1 0.0 copy-start.10
  3.1 0.9 %copy-done.10 = f32[32,1024]{1,0:T(8,128)S(1)} copy-done((f32[32,1024]{1,0:T(8,128)S(1)}, f32[32,1024]{1,0:T(8,128)}, u32[]{:S(2)}) %copy-start.10) | copy-done | bytes 131096
  4.0 0.0 copy-start.12
  4.0 0.9 %copy-done.12 = f32[32,1024]{1,0:T(8,128)S(1)} copy-done((f32[32,1024]{1,0:T(8,128)S(1)}, f32[32,1024]{1,0:T(8,128)}, u32[]{:S(2)}) %copy-start.12) | copy-done | bytes 131096
  4.9 0.0 copy-start.14
  5.0 0.8 copy-done.14
  5.7 0.0 copy-start.15
  5.7 0.0 copy-start.17
  5.7 0.0 copy-start.7
  5.7 0.0 copy-start.9
  5.7 0.0 copy-start.11
  5.7 0.0 copy-start.13
  5.7 10.7 %end_state.1 = bf16[16,144,128]{2,1,0:T(8,128)(2,1)} custom-call(bf16[1024,2048]{1,0:T(8,128)(2,1)S(1)} %copy-done, f32[4,2048]{1,0:T(4,128)S(1)} %copy-done.14, bf16[1024,128]{1,0:T(8,128)(2,1)S(1)} %copy-done.8, f32[32,1024]{1,0:T(8,128)S(1)} %copy-done.10, f32[32,1024]{1,0:T(8,128)S(1)} %copy-done.12), custom_call_target="tpu_custom_call" | custom-call | tf_op jit(solution)/shard_map/end_state/pallas_call | solution.py:165
  16.4 8.1 %all-to-all-start = ((bf16[16,144,128]{2,1,0:T(8,128)(2,1)}), bf16[16,144,128]{2,1,0:T(8,128)(2,1)S(1)}, u32[]{:S(2)}, u32[]{:S(2)}) async-start(bf16[16,144,128]{2,1,0:T(8,128)(2,1)} %end_state.1), calls=%async_computation | async-start | bytes 1179648 | tf_op jit(solution)/shard_map/all_to_all | solution.py:440
  24.6 0.8 slice.3
  25.4 3.8 %collective-permute-start = (bf16[16,2048]{1,0:T(8,128)(2,1)S(1)}, bf16[16,2048]{1,0:T(8,128)(2,1)S(1)}, u32[]{:S(2)}, u32[]{:S(2)}) collective-permute-start(bf16[16,2048]{1,0:T(8,128)(2,1)S(1)} %slice.3), channel_id=1, source_target_pairs={{0,8},{8,16},{16,24},{24,32},{32,40},{40,48},{48,56},{56,64},{64,7... | collective-permute-start | bytes 196616 | tf_op jit(solution)/shard_map/ppermute | solution.py:442
  29.2 0.0 copy-done.15
  29.3 7.4 %all-to-all-done.in_ref = bf16[16,144,128]{2,1,0:T(8,128)(2,1)S(1)} async-done(((bf16[16,144,128]{2,1,0:T(8,128)(2,1)}), bf16[16,144,128]{2,1,0:T(8,128)(2,1)S(1)}, u32[]{:S(2)}, u32[]{:S(2)}) %all-to-all-start) | async-done | bytes 589856 | tf_op jit(solution)/shard_map/all_to_all | solution.py:440
  36.7 1.8 %prefix.1 = bf16[16,144,128]{2,1,0:T(8,128)(2,1)} custom-call(bf16[16,144,128]{2,1,0:T(8,128)(2,1)S(1)} %all-to-all-done.in_ref, f32[4,128]{1,0:T(4,128)S(1)} %constant_dynamic-slice_fusion.weight_ref), custom_call_target="tpu_custom_call" | custom-call | tf_op jit(solution)/shard_map/prefix/pallas_call | solution.py:237
  38.5 0.0 collective-permute-done.halo_ref
  38.5 3.9 %all-to-all-start.1 = ((bf16[16,144,128]{2,1,0:T(8,128)(2,1)}), bf16[16,144,128]{2,1,0:T(8,128)(2,1)S(1)}, u32[]{:S(2)}, u32[]{:S(2)}) async-start(bf16[16,144,128]{2,1,0:T(8,128)(2,1)} %prefix.1), calls=%async_computation.1 | async-start | bytes 1179648 | tf_op jit(solution)/shard_map/all_to_all | solution.py:446
  42.4 0.0 copy-done.17
  42.4 0.1 copy.10.skip_ref
  42.5 0.0 copy-done.7
  42.5 0.0 copy-done.9
  42.5 0.0 copy-done.11
  42.5 0.0 copy-done.13
  42.5 0.0 copy-start.1
  42.5 2.2 %copy-done.1 = bf16[1024,2048]{1,0:T(8,128)(2,1)S(1)} copy-done((bf16[1024,2048]{1,0:T(8,128)(2,1)S(1)}, bf16[1024,2048]{1,0:T(8,128)(2,1)}, u32[]{:S(2)}) %copy-start.1) | copy-done | bytes 4194328
  44.7 0.0 copy-start.6
  44.7 2.2 %copy-done.6 = bf16[1024,2048]{1,0:T(8,128)(2,1)S(1)} copy-done((bf16[1024,2048]{1,0:T(8,128)(2,1)S(1)}, bf16[1024,2048]{1,0:T(8,128)(2,1)}, u32[]{:S(2)}) %copy-start.6) | copy-done | bytes 4194328
  46.9 0.0 copy-start.16
  46.9 21.4 %local_part.1 = (f32[1024,2048]{1,0:T(8,128)S(1)}, f32[1024,2048]{1,0:T(8,128)S(1)}) custom-call(bf16[1024,2048]{1,0:T(8,128)(2,1)S(1)} %copy-done.1, bf16[16,2048]{1,0:T(8,128)(2,1)S(1)} %collective-permute-done.halo_ref, f32[4,2048]{1,0:T(4,128)S(1)} %copy-done.15, bf16[1024,2048]{1,0:T(8,128)(2,1)S(1)} %copy-done.6, bf16[1024,128]{1,0:T(8,128)(2,1)S(1)} %copy-done.9, ...), custom_call_target="tpu_custom_call" | custom-call | tf_op jit(solution)/shard_map/local_part/pallas_call | solution.py:347
  68.3 0.0 copy-start.2
  68.3 3.2 %copy-done.2 = f32[1024,2048]{1,0:T(8,128)} copy-done((f32[1024,2048]{1,0:T(8,128)}, f32[1024,2048]{1,0:T(8,128)S(1)}, u32[]{:S(2)}) %copy-start.2) | copy-done | bytes 8388632
  71.5 0.0 copy-start.4
  71.5 3.2 %copy-done.4 = f32[1024,2048]{1,0:T(8,128)} copy-done((f32[1024,2048]{1,0:T(8,128)}, f32[1024,2048]{1,0:T(8,128)S(1)}, u32[]{:S(2)}) %copy-start.4) | copy-done | bytes 8388632
  74.8 0.0 all-to-all-done.1.state_ref
  74.8 0.0 copy-done.16
  74.8 0.0 copy-start.3
  74.8 3.4 %copy-done.3 = f32[1024,2048]{1,0:T(8,128)S(1)} copy-done((f32[1024,2048]{1,0:T(8,128)S(1)}, f32[1024,2048]{1,0:T(8,128)}, u32[]{:S(2)}) %copy-start.3) | copy-done | bytes 8388632
  78.1 0.0 copy-start.5
  78.1 3.4 %copy-done.5 = f32[1024,2048]{1,0:T(8,128)S(1)} copy-done((f32[1024,2048]{1,0:T(8,128)S(1)}, f32[1024,2048]{1,0:T(8,128)}, u32[]{:S(2)}) %copy-start.5) | copy-done | bytes 8388632
  81.5 6.0 %final_part.1 = bf16[1024,2048]{1,0:T(8,128)(2,1)} custom-call(bf16[16,144,128]{2,1,0:T(8,128)(2,1)S(1)} %all-to-all-done.1.state_ref, bf16[1024,128]{1,0:T(8,128)(2,1)S(1)} %copy-done.7, f32[1024,2048]{1,0:T(8,128)S(1)} %copy-done.3, f32[1024,2048]{1,0:T(8,128)S(1)} %copy-done.5, f32[1,2048]{1,0:T(1,128)S(1)} %bitcast.2), custom_call_target="tpu_custom_call" | custom-call | tf_op jit(solution)/shard_map/final_part/pallas_call | solution.py:414
  (1 shorter events, 0.0 us)
Async XLA Ops:
  0.0 2.2 %copy-start = (bf16[1024,2048]{1,0:T(8,128)(2,1)S(1)}, bf16[1024,2048]{1,0:T(8,128)(2,1)}, u32[]{:S(2)}) copy-start(bf16[1024,2048]{1,0:T(8,128)(2,1)} %x_ref.3) | copy-start | bytes 12582916
  2.2 0.9 %copy-start.8 = (bf16[1024,128]{1,0:T(8,128)(2,1)S(1)}, bf16[1024,128]{1,0:T(8,128)(2,1)}, u32[]{:S(2)}) copy-start(bf16[1024,128]{1,0:T(8,128)(2,1)} %write_ref.3) | copy-start | bytes 786436
  3.1 0.9 %copy-start.10 = (f32[32,1024]{1,0:T(8,128)S(1)}, f32[32,1024]{1,0:T(8,128)}, u32[]{:S(2)}) copy-start(f32[32,1024]{1,0:T(8,128)} %step_ref.3) | copy-start | bytes 393220
  4.0 0.9 %copy-start.12 = (f32[32,1024]{1,0:T(8,128)S(1)}, f32[32,1024]{1,0:T(8,128)}, u32[]{:S(2)}) copy-start(f32[32,1024]{1,0:T(8,128)} %decay_ref.3) | copy-start | bytes 393220
  4.9 0.8 copy-start.14
  5.7 23.5 %copy-start.15 = (f32[4,2048]{1,0:T(4,128)S(1)}, f32[4,2048]{1,0:T(4,128)}, u32[]{:S(2)}) copy-start(f32[4,2048]{1,0:T(4,128)} %weight_ref.3) | copy-start | bytes 98308
  5.7 36.7 %copy-start.17 = (f32[32]{0:T(128)S(1)}, f32[32]{0:T(128)}, u32[]{:S(2)}) copy-start(f32[32]{0:T(128)} %param.16) | copy-start | bytes 388
  5.7 36.8 %copy-start.7 = (bf16[1024,128]{1,0:T(8,128)(2,1)S(1)}, bf16[1024,128]{1,0:T(8,128)(2,1)}, u32[]{:S(2)}) copy-start(bf16[1024,128]{1,0:T(8,128)(2,1)} %read_ref.3) | copy-start | bytes 786436
  5.7 36.8 %copy-start.9 = (bf16[1024,128]{1,0:T(8,128)(2,1)S(1)}, bf16[1024,128]{1,0:T(8,128)(2,1)}, u32[]{:S(2)}) copy-start(bf16[1024,128]{1,0:T(8,128)(2,1)} %write_ref.3) | copy-start | bytes 786436
  5.7 36.8 %copy-start.11 = (f32[32,1024]{1,0:T(8,128)S(1)}, f32[32,1024]{1,0:T(8,128)}, u32[]{:S(2)}) copy-start(f32[32,1024]{1,0:T(8,128)} %step_ref.3) | copy-start | bytes 393220
  5.7 36.8 %copy-start.13 = (f32[32,1024]{1,0:T(8,128)S(1)}, f32[32,1024]{1,0:T(8,128)}, u32[]{:S(2)}) copy-start(f32[32,1024]{1,0:T(8,128)} %decay_ref.3) | copy-start | bytes 393220
  16.4 20.3 %all-to-all-start = ((bf16[16,144,128]{2,1,0:T(8,128)(2,1)}), bf16[16,144,128]{2,1,0:T(8,128)(2,1)S(1)}, u32[]{:S(2)}, u32[]{:S(2)}) async-start(bf16[16,144,128]{2,1,0:T(8,128)(2,1)} %end_state.1), calls=%async_computation | async-start | bytes 1179648 | tf_op jit(solution)/shard_map/all_to_all | solution.py:440
  25.4 13.1 %collective-permute-start = (bf16[16,2048]{1,0:T(8,128)(2,1)S(1)}, bf16[16,2048]{1,0:T(8,128)(2,1)S(1)}, u32[]{:S(2)}, u32[]{:S(2)}) collective-permute-start(bf16[16,2048]{1,0:T(8,128)(2,1)S(1)} %slice.3), channel_id=1, source_target_pairs={{0,8},{8,16},{16,24},{24,32},{32,40},{40,48},{48,56},{56,64},{64,7... | collective-permute-start | bytes 196616 | tf_op jit(solution)/shard_map/ppermute | solution.py:442
  38.5 36.2 %all-to-all-start.1 = ((bf16[16,144,128]{2,1,0:T(8,128)(2,1)}), bf16[16,144,128]{2,1,0:T(8,128)(2,1)S(1)}, u32[]{:S(2)}, u32[]{:S(2)}) async-start(bf16[16,144,128]{2,1,0:T(8,128)(2,1)} %prefix.1), calls=%async_computation.1 | async-start | bytes 1179648 | tf_op jit(solution)/shard_map/all_to_all | solution.py:446
  42.5 2.2 %copy-start.1 = (bf16[1024,2048]{1,0:T(8,128)(2,1)S(1)}, bf16[1024,2048]{1,0:T(8,128)(2,1)}, u32[]{:S(2)}) copy-start(bf16[1024,2048]{1,0:T(8,128)(2,1)} %x_ref.3) | copy-start | bytes 12582916
  44.7 2.2 %copy-start.6 = (bf16[1024,2048]{1,0:T(8,128)(2,1)S(1)}, bf16[1024,2048]{1,0:T(8,128)(2,1)}, u32[]{:S(2)}) copy-start(bf16[1024,2048]{1,0:T(8,128)(2,1)} %gate_ref.1) | copy-start | bytes 12582916
  46.9 27.9 %copy-start.16 = (f32[2048]{0:T(1024)S(1)}, f32[2048]{0:T(1024)}, u32[]{:S(2)}) copy-start(f32[2048]{0:T(1024)} %param.17) | copy-start | bytes 24580
  68.3 3.3 %copy-start.2 = (f32[1024,2048]{1,0:T(8,128)}, f32[1024,2048]{1,0:T(8,128)S(1)}, u32[]{:S(2)}) copy-start(f32[1024,2048]{1,0:T(8,128)S(1)} %get-tuple-element.13.own_ref) | copy-start | bytes 25165828
  71.5 3.2 %copy-start.4 = (f32[1024,2048]{1,0:T(8,128)}, f32[1024,2048]{1,0:T(8,128)S(1)}, u32[]{:S(2)}) copy-start(f32[1024,2048]{1,0:T(8,128)S(1)} %get-tuple-element.14.reach_ref) | copy-start | bytes 25165828
  74.8 3.4 %copy-start.3 = (f32[1024,2048]{1,0:T(8,128)S(1)}, f32[1024,2048]{1,0:T(8,128)}, u32[]{:S(2)}) copy-start(f32[1024,2048]{1,0:T(8,128)} %copy-done.2) | copy-start | bytes 25165828
  78.1 3.4 %copy-start.5 = (f32[1024,2048]{1,0:T(8,128)S(1)}, f32[1024,2048]{1,0:T(8,128)}, u32[]{:S(2)}) copy-start(f32[1024,2048]{1,0:T(8,128)} %copy-done.4) | copy-start | bytes 25165828

commit v2 on v0

v2 whole, which is shorter than its diff:
```python
import functools

import jax
import jax.numpy as jnp
from jax import lax
from jax.experimental import pallas as pl
from jax.experimental.pallas import tpu as pltpu
from jax.sharding import PartitionSpec as P

F32 = jnp.float32
BF16 = jnp.bfloat16
HEAD = 64
STATE = 128
TAPS = 4
CHUNK = 128
LANES = 256
EXTRA = 16
HIGHEST = lax.Precision.HIGHEST
VMEM_BYTES = 24 * 1024 * 1024


def iota(shape, dim):
    return lax.broadcasted_iota(jnp.int32, shape, dim)


def dot(a, b):
    return jnp.dot(a, b, preferred_element_type=F32)


def dot_exact(a, b):
    return jnp.dot(a, b, preferred_element_type=F32, precision=HIGHEST)


def split(value):
    high = value.astype(BF16)
    return high, (value - high.astype(F32)).astype(BF16)


def silu_of_half(half):
    return half * jnp.tanh(half) + half


def encode(value):
    top = jnp.max(jnp.abs(value), axis=0, keepdims=True)
    scale = jnp.maximum(top * 1.00390625, 1e-30).astype(BF16).astype(F32)
    size = jnp.exp2(jnp.abs(value) * (252.0 / scale) - 126.0)
    return jnp.where(value < 0, -size, size).astype(BF16), scale


def decode(code, scale):
    code = code.astype(F32)
    size = (jnp.log2(jnp.abs(code)) + 126.0) * (scale * (1.0 / 252.0))
    return jnp.where(code < 0, -size, size)


def stack_chunks(value):
    pieces = value.shape[1] // CHUNK
    return jnp.concatenate([value[:, CHUNK * c : CHUNK * (c + 1)] for c in range(pieces)], axis=0)


def head_spread(heads, channels):
    return (iota((heads, channels), 0) == iota((heads, channels), 1) // HEAD).astype(F32)


def store_tokens(ref, value, heads):
    for c in range(value.shape[0] // heads):
        part = value[heads * c : heads * (c + 1)]
        high = part.astype(BF16).astype(F32)
        both = jnp.concatenate([high, part - high], axis=0)
        ref[CHUNK * c : CHUNK * (c + 1), :] = both.T.astype(BF16)


def conv_half(rows, weight):
    weight = weight * 0.5
    back = pltpu.roll(rows, 1, 0)
    near = rows * weight[3:4] + back * weight[2:3]
    far = rows * weight[1:2] + back * weight[0:1]
    return (near + pltpu.roll(far, 2, 0))[16:]


def conv_silu(stage, part, start, count, weight):
    half = stage[part, pl.ds(start + 8, count)] * weight[3:4]
    for back in range(1, TAPS):
        half = half + stage[part, pl.ds(start + 8 - back, count)] * weight[3 - back : 4 - back]
    return silu_of_half(half)


def end_state_kernel(
    x_hbm, weight_hbm, write_hbm, step_hbm, decay_hbm, out_hbm, value_hbm,
    x_ref, weight_ref, write_ref, step_ref, decay_ref, gains, spread, keys, packed, stage, out_ref, value_ref, sems,
):
    heads, tokens = step_ref.shape
    pieces = tokens // CHUNK
    channels = heads * HEAD
    turns = channels // LANES
    small = [
        pltpu.make_async_copy(source, target, sems.at[turns + i])
        for i, (source, target) in enumerate(
            ((decay_hbm, decay_ref), (step_hbm, step_ref), (write_hbm, write_ref), (weight_hbm, weight_ref))
        )
    ]

    def fetch(turn):
        lanes = pl.ds(pl.multiple_of(turn * LANES, LANES), LANES)
        return pltpu.make_async_copy(x_hbm.at[:, lanes], x_ref.at[:, lanes], sems.at[turn])

    def leave(turn):
        lanes = pl.ds(pl.multiple_of(turn * LANES, LANES), LANES)
        return pltpu.make_async_copy(
            value_ref.at[turn], value_hbm.at[:, lanes], sems.at[2 * turns + 4 + turn]
        )

    def leave_code(turn):
        places = pl.ds(turn * (LANES // 128), LANES // 128)
        return pltpu.make_async_copy(out_ref.at[places], out_hbm.at[places], sems.at[turns + 4 + turn])

    for copy in small:
        copy.start()
    for turn in range(turns):
        fetch(turn).start()
    ones = head_spread(heads, channels)
    spread[...] = jnp.concatenate([ones, ones], axis=0).astype(BF16)
    for part in range(LANES // 128):
        stage[part, 0:8] = jnp.zeros((8, 128), F32)
    small[0].wait()
    small[1].wait()
    decay = decay_ref[...]
    logs = stack_chunks(decay)
    later = (iota((CHUNK, CHUNK), 0) > iota((CHUNK, CHUNK), 1)).astype(F32)
    suffix = dot_exact(logs, later)
    total = suffix[:, 0:1] + logs[:, 0:1]
    offset = jnp.zeros((heads, 1), F32)
    offsets = []
    for c in reversed(range(pieces)):
        offsets.append(offset)
        offset = offset + total[heads * c : heads * (c + 1)]
    suffix = suffix + jnp.concatenate(offsets[::-1], axis=0)
    gain = jnp.exp(suffix) * stack_chunks(step_ref[...])
    row, lane = (iota(gain.shape, 0), iota(gain.shape, 1))
    gain = jnp.where((row < heads) & (lane < TAPS - 1), 0.0, gain)
    store_tokens(gains, gain, heads)
    first = decay[:, 0:CHUNK]
    lane = iota(first.shape, 1)
    run0 = first[:, 0:1]
    run1 = run0 + first[:, 1:2]
    run2 = run1 + first[:, 2:3]
    step = step_ref[:, 0:CHUNK]
    scalars = jnp.where(lane == 0, jnp.exp(offset), 0.0)
    for t, run in enumerate((run0, run1, run2)):
        scalars = jnp.where(lane == t + 1, jnp.exp(-run) * step[:, t : t + 1], scalars)
    wide = dot_exact(scalars.T[0:8], ones)
    segment = (iota(wide.shape, 1) % HEAD) // (HEAD // 4)
    packed[...] = jnp.broadcast_to(
        jnp.sum(jnp.where(iota(wide.shape, 0) == segment, wide, 0.0), axis=0, keepdims=True),
        packed.shape,
    )
    small[2].wait()
    small[3].wait()
    write_t = write_ref[...].astype(F32).T.astype(BF16)
    for c in range(pieces):
        part = write_t[:, CHUNK * c : CHUNK * (c + 1)]
        keys[CHUNK * c : CHUNK * (c + 1)] = jnp.concatenate([part, part], axis=1)

    def weigh(turn):
        lanes = pl.ds(pl.multiple_of(turn * LANES, LANES), LANES)
        fetch(turn).wait()
        weight = weight_ref[:, lanes] * 0.5
        state = jnp.zeros((STATE, LANES), F32)
        for c in range(pieces):
            span = slice(CHUNK * c, CHUNK * (c + 1))
            rows = x_ref[span, lanes].astype(F32)
            gain = dot(gains[span], spread[:, lanes])
            sides = []
            for part in range(LANES // 128):
                cols = slice(128 * part, 128 * (part + 1))
                stage[part, 8 + CHUNK * c : 8 + CHUNK * (c + 1)] = rows[:, cols]
                value = conv_silu(stage, part, CHUNK * c, CHUNK, weight[:, cols])
                value_ref[turn, span, cols] = value
                sides.append(jnp.concatenate(split(value * gain[:, cols]), axis=0))
            state = state + dot(keys[span], jnp.concatenate(sides, axis=1))
        leave(turn).start()
        return state

    def finish(turn, state):
        lanes = pl.ds(pl.multiple_of(turn * LANES, LANES), LANES)
        code, scale = encode(state)
        row = iota((EXTRA, LANES), 0)
        first = pltpu.roll(x_ref[0:16, lanes].astype(F32), 7, 0)
        last = pltpu.roll(x_ref[tokens - 16 : tokens, lanes].astype(F32), 7, 0)
        writes = pltpu.roll(write_ref[0:16].astype(F32), 1, 0)
        writes = jnp.concatenate([writes] * (LANES // STATE), axis=1)
        scalar = packed[0:1, lanes]
        high = scalar.astype(BF16).astype(F32)
        middle = (scalar - high).astype(BF16).astype(F32)
        low = scalar - high - middle
        extra = jnp.where(row == 0, scale, 0.0)
        extra = jnp.where((row >= 1) & (row <= 3), writes, extra)
        extra = jnp.where((row >= 4) & (row <= 6), last, extra)
        extra = jnp.where((row >= 7) & (row <= 9), first, extra)
        extra = jnp.where(row == 10, high, extra)
        extra = jnp.where(row == 11, middle, extra)
        extra = jnp.where(row == 12, low, extra).astype(BF16)
        for part in range(LANES // 128):
            place = turn * (LANES // 128) + part
            out_ref[place, 0:STATE] = code[:, 128 * part : 128 * (part + 1)]
            out_ref[place, STATE : STATE + EXTRA] = extra[:, 128 * part : 128 * (part + 1)]

    def pair(i, carry):
        for side in range(2):
            turn = 2 * i + side
            finish(turn, weigh(turn))
            leave_code(turn).start()
        return carry

    lax.fori_loop(0, turns // 2, pair, 0)
    for turn in range(turns):
        leave(turn).wait()
        leave_code(turn).wait()


def in_hbm(*values):
    return [pltpu.with_memory_space_constraint(value, pltpu.HBM) for value in values]


def end_state(x, weight, write, step, decay):
    tokens, channels = x.shape
    heads = step.shape[0]
    owners = channels // 128
    return pl.pallas_call(
        end_state_kernel,
        in_specs=[pl.BlockSpec(memory_space=pltpu.HBM)] * 5,
        out_specs=[pl.BlockSpec(memory_space=pltpu.HBM)] * 2,
        out_shape=[pltpu.HBM((owners, STATE + EXTRA, 128), BF16), pltpu.HBM((tokens, channels), F32)],
        scratch_shapes=[
            pltpu.VMEM(x.shape, BF16),
            pltpu.VMEM(weight.shape, F32),
            pltpu.VMEM(write.shape, BF16),
            pltpu.VMEM(step.shape, F32),
            pltpu.VMEM(decay.shape, F32),
            pltpu.VMEM((tokens, 2 * heads), BF16),
            pltpu.VMEM((2 * heads, channels), BF16),
            pltpu.VMEM((tokens, 2 * CHUNK), BF16),
            pltpu.VMEM((8, channels), F32),
            pltpu.VMEM((LANES // 128, 8 + tokens, 128), F32),
            pltpu.VMEM((owners, STATE + EXTRA, 128), BF16),
            pltpu.VMEM((channels // LANES, tokens, LANES), F32),
            pltpu.SemaphoreType.DMA((3 * (channels // LANES) + 4,)),
        ],
        compiler_params=pltpu.CompilerParams(vmem_limit_bytes=VMEM_BYTES),
        name="end_state",
    )(*in_hbm(x, weight, write, step, decay))


def prefix_kernel(place_ref, in_ref, weight_ref, out_ref, blocks):
    count = in_ref.shape[0]
    tile = in_ref[:, STATE : STATE + EXTRA, :].astype(F32)
    shape = tile.shape
    row, lane = (iota(shape, 1), iota(shape, 2))
    before = jnp.concatenate([jnp.zeros((1,) + shape[1:], F32), tile[:-1]], axis=0)
    rows = jnp.where(
        (row >= 4) & (row <= 6), before, jnp.where((row >= 7) & (row <= 9), tile, 0.0)
    )
    weight = weight_ref[:, pl.ds(pl.multiple_of(place_ref[0] * 128, 128), 128)] * 0.5
    half = rows * weight[3:4][None]
    for back in range(1, TAPS):
        half = half + pltpu.roll(rows, back, 1) * weight[3 - back : 4 - back][None]
    value = silu_of_half(half)
    scalars = jnp.sum(jnp.where((row >= 10) & (row <= 12), tile, 0.0), axis=1, keepdims=True)
    left = iota(scalars.shape, 2) < HEAD

    def spread_of(segment):
        place = segment * (HEAD // 4)
        return jnp.where(
            left, scalars[:, :, place : place + 1], scalars[:, :, HEAD + place : HEAD + place + 1]
        )

    fade = spread_of(0)
    gain = jnp.where(row == 7, spread_of(1), jnp.where(row == 8, spread_of(2), spread_of(3)))
    coarse = value.astype(BF16).astype(F32)
    firsts = jnp.where(row <= 3, pltpu.roll(coarse, EXTRA - 6, 1), pltpu.roll(value - coarse, EXTRA - 3, 1))
    value = jnp.where((row >= 7) & (row <= 9), value * gain, 0.0)
    value = pltpu.roll(value, EXTRA - 6, 1)
    high = value.astype(BF16)
    low = (value - high.astype(F32)).astype(BF16)
    keys = jnp.where((row >= 1) & (row <= 3), tile, 0.0).reshape(count * EXTRA, 128).T.astype(BF16)
    blocks[...] = jnp.zeros(blocks.shape, BF16)
    for j in range(count):
        blocks[EXTRA * j : EXTRA * (j + 1), 128 * j : 128 * (j + 1)] = high[j]
        blocks[EXTRA * (count + j) : EXTRA * (count + j + 1), 128 * j : 128 * (j + 1)] = low[j]
    first = dot(jnp.concatenate([keys, keys], axis=1), blocks[...])
    state = jnp.zeros((STATE, 128), F32)
    top_row = iota((EXTRA, 128), 0) == 0
    for j in range(count):
        state = state + first[:, 128 * j : 128 * (j + 1)]
        code, scale = encode(state)
        out_ref[j, 0:STATE] = code
        out_ref[j, STATE : STATE + EXTRA] = jnp.where(top_row, scale, firsts[j]).astype(BF16)
        local = decode(in_ref[j, 0:STATE], tile[j, 0:1])
        state = fade[j] * state + local


def prefix(place, received, weight):
    count = received.shape[0]
    whole = pl.BlockSpec(memory_space=pltpu.VMEM)
    return pl.pallas_call(
        prefix_kernel,
        in_specs=[pl.BlockSpec(memory_space=pltpu.SMEM), whole, whole],
        out_specs=whole,
        out_shape=jax.ShapeDtypeStruct(received.shape, BF16),
        scratch_shapes=[pltpu.VMEM((2 * count * EXTRA, count * 128), BF16)],
        compiler_params=pltpu.CompilerParams(vmem_limit_bytes=VMEM_BYTES),
        name="prefix",
    )(place, received, weight)


def local_tables_kernel(
    write_hbm, read_hbm, step_hbm, decay_hbm, skip_ref, gains_out, fades_out, reach_out, keys_out, mix_out, rowed_out,
    write_ref, read_ref, step_ref, decay_ref, gains, fades, reach, keys, mix, rowed, sems,
):
    heads, tokens = step_ref.shape
    pieces = tokens // CHUNK
    channels = heads * HEAD
    moves = [
        pltpu.make_async_copy(source, target, sems.at[i])
        for i, (source, target) in enumerate(
            (
                (decay_hbm, decay_ref), (step_hbm, step_ref), (write_hbm, write_ref), (read_hbm, read_ref),
                (gains, gains_out), (fades, fades_out), (reach, reach_out), (keys, keys_out), (mix, mix_out),
                (rowed, rowed_out),
            )
        )
    ]
    for copy in moves[:4]:
        copy.start()
    ones = head_spread(heads, channels)
    for copy in moves[:4]:
        copy.wait()
    logs = stack_chunks(decay_ref[...])
    upto = (iota((CHUNK, CHUNK), 0) <= iota((CHUNK, CHUNK), 1)).astype(F32)
    run = dot_exact(logs, upto)
    middle = run[:, CHUNK // 2 - 1 : CHUNK // 2]
    total = run[:, CHUNK - 1 : CHUNK]
    gain = jnp.exp(middle - run) * stack_chunks(step_ref[...])
    gain = jnp.where((iota(gain.shape, 0) < heads) & (iota(gain.shape, 1) < TAPS - 1), 0.0, gain)
    store_tokens(gains, gain, heads)
    store_tokens(fades, jnp.exp(run - middle), heads)
    lane = iota((heads, 128), 1)
    scalars = jnp.where(lane == pieces, skip_ref[...], 0.0)
    offset = jnp.zeros((heads, 1), F32)
    offsets = []
    for c in range(pieces):
        offsets.append(offset)
        mid = middle[heads * c : heads * (c + 1)]
        tot = total[heads * c : heads * (c + 1)]
        offset = offset + tot
        if c + 1 < pieces:
            onward = jnp.exp(middle[heads * (c + 1) : heads * (c + 2)] + (tot - mid))
            scalars = jnp.where(lane == c, onward, scalars)
    store_tokens(reach, jnp.exp(run + jnp.concatenate(offsets, axis=0)), heads)
    causal = iota((CHUNK, CHUNK), 0) >= iota((CHUNK, CHUNK), 1)
    for c in range(pieces):
        span = slice(CHUNK * c, CHUNK * (c + 1))
        write = write_ref[span]
        read = read_ref[span]
        mixing = lax.dot_general(read, write, (((1,), (1,)), ((), ())), preferred_element_type=F32)
        if c == 0:
            place = pieces + 1
            for t, later in ((0, 1), (0, 2), (1, 2)):
                weight = jnp.exp(run[0:heads, t : t + 1] - run[0:heads, later : later + 1])
                weight = weight * step_ref[:, later : later + 1] * mixing[t : t + 1, later : later + 1]
                scalars = jnp.where(lane == place, weight, scalars)
                place += 1
        high, low = split(jnp.where(causal, mixing, 0.0))
        mix[span] = jnp.concatenate([high, high, low, read, read], axis=1)
        write_t = write.astype(F32).T.astype(BF16)
        keys[span] = jnp.concatenate([write_t, write_t], axis=1)
    rowed[...] = dot_exact(scalars.T[0 : rowed.shape[0]], ones)
    for copy in moves[4:]:
        copy.start()
    for copy in moves[4:]:
        copy.wait()


def local_tables(write, read, step, decay, skip):
    heads, tokens = step.shape
    pieces = tokens // CHUNK
    channels = heads * HEAD
    hbm = pl.BlockSpec(memory_space=pltpu.HBM)
    outs = [
        ((tokens, 2 * heads), BF16),
        ((tokens, 2 * heads), BF16),
        ((tokens, 2 * heads), BF16),
        ((tokens, 2 * CHUNK), BF16),
        ((tokens, 5 * CHUNK), BF16),
        ((pieces + 8, channels), F32),
    ]
    ins = (write, read, step, decay)
    return pl.pallas_call(
        local_tables_kernel,
        in_specs=[hbm] * 4 + [pl.BlockSpec(memory_space=pltpu.VMEM)],
        out_specs=[hbm] * len(outs),
        out_shape=[pltpu.HBM(*out) for out in outs],
        scratch_shapes=[pltpu.VMEM(value.shape, value.dtype) for value in ins]
        + [pltpu.VMEM(*out) for out in outs]
        + [pltpu.SemaphoreType.DMA((len(ins) + len(outs),))],
        compiler_params=pltpu.CompilerParams(vmem_limit_bytes=VMEM_BYTES),
        name="local_tables",
    )(*in_hbm(*ins), skip)


def local_kernel(
    begin, value_hbm, gains_hbm, fades_hbm, keys_hbm, mix_hbm, rowed_hbm, local_hbm,
    value_ref, gains, fades, keys, mix, rowed, spread, gain0, gain1, fade0, fade1, result, sems,
):
    tokens, width = local_hbm.shape
    pieces = tokens // CHUNK
    channels = rowed.shape[1]
    turns = width // LANES
    wide_gains, wide_fades = (gain0, gain1), (fade0, fade1)
    pairs = (
        (gains_hbm, gains), (keys_hbm, keys), (mix_hbm, mix), (rowed_hbm, rowed), (fades_hbm, fades)
    )
    small = [
        pltpu.make_async_copy(source, target, sems.at[2 * turns + i])
        for i, (source, target) in enumerate(pairs)
    ]

    def columns(turn):
        return pl.ds(pl.multiple_of(turn * LANES, LANES), LANES)

    def fetch(turn):
        return pltpu.make_async_copy(
            value_hbm.at[:, columns(turn + begin)], value_ref.at[turn], sems.at[turn]
        )

    def leave(turn):
        return pltpu.make_async_copy(
            result.at[turn], local_hbm.at[:, columns(turn)], sems.at[turns + turn]
        )

    def widen(turn, side):
        lanes = columns(turn + begin)
        wide_gains[side][...] = dot(gains[...], spread[:, lanes])
        wide_fades[side][...] = dot(fades[...], spread[:, lanes])

    small[0].start()
    fetch(0).start()
    for copy in small[1:]:
        copy.start()
    for turn in range(1, turns):
        fetch(turn).start()
    ones = head_spread(channels // HEAD, channels)
    spread[...] = jnp.concatenate([ones, ones], axis=0).astype(BF16)
    for copy in small:
        copy.wait()
    widen(0, 0)

    def work(turn, side):
        lanes = columns(turn + begin)
        fetch(turn).wait()
        skip = rowed[pieces : pieces + 1, lanes]
        widen(jnp.minimum(turn + 1, turns - 1), 1 - side)
        state = None
        for c in range(pieces):
            span = slice(CHUNK * c, CHUNK * (c + 1))
            both = jnp.concatenate(split(value_ref[turn, span] * wide_gains[side][span]), axis=0)
            if state is None:
                mixed = dot(mix[span, 0 : 3 * CHUNK], jnp.concatenate([both, both[0:CHUNK]], axis=0))
                state = dot(keys[span], both)
            else:
                high, low = split(state)
                mixed = dot(mix[span], jnp.concatenate([both, both[0:CHUNK], high, low], axis=0))
                if c + 1 < pieces:
                    state = state + dot(keys[span], both)
            if c + 1 < pieces:
                state = state * rowed[c : c + 1, lanes]
            result[turn, span] = mixed * wide_fades[side][span] + skip * value_ref[turn, span]
        leave(turn).start()

    def pair(i, carry):
        for side in range(2):
            work(2 * i + side, side)
        return carry

    lax.fori_loop(0, turns // 2, pair, 0)
    for turn in range(turns):
        leave(turn).wait()


def local_part(begin, turns, value, gains, fades, keys, mix, rowed):
    tokens, channels = value.shape
    hbm = pl.BlockSpec(memory_space=pltpu.HBM)
    inputs = in_hbm(value, gains, fades, keys, mix, rowed)
    return pl.pallas_call(
        functools.partial(local_kernel, begin),
        in_specs=[hbm] * 6,
        out_specs=hbm,
        out_shape=pltpu.HBM((tokens, turns * LANES), F32),
        scratch_shapes=[
            pltpu.VMEM((turns, tokens, LANES), F32),
            pltpu.VMEM(gains.shape, BF16),
            pltpu.VMEM(fades.shape, BF16),
            pltpu.VMEM(keys.shape, BF16),
            pltpu.VMEM(mix.shape, BF16),
            pltpu.VMEM(rowed.shape, F32),
            pltpu.VMEM((2 * (channels // HEAD), channels), BF16),
            pltpu.VMEM((tokens, LANES), F32),
            pltpu.VMEM((tokens, LANES), F32),
            pltpu.VMEM((tokens, LANES), F32),
            pltpu.VMEM((tokens, LANES), F32),
            pltpu.VMEM((turns, tokens, LANES), F32),
            pltpu.SemaphoreType.DMA((2 * turns + 5,)),
        ],
        compiler_params=pltpu.CompilerParams(vmem_limit_bytes=VMEM_BYTES),
        name="local_part",
    )(*inputs)


def final_kernel(
    state_ref, gain_ref, read_hbm, fade_hbm, rowed_hbm, left_hbm, right_hbm, gate_hbm, out_hbm,
    read_ref, fade_ref, rowed, local_ref, gate_ref, states, spread, gated, out_ref, sems,
):
    owners = state_ref.shape[0]
    channels = owners * 128
    tokens = read_ref.shape[0]
    heads = channels // HEAD
    turns = tokens // CHUNK

    def rows(turn):
        return pl.ds(pl.multiple_of(turn * CHUNK, CHUNK), CHUNK)

    def fetch(turn):
        half = left_hbm.shape[1]
        moves = (
            (left_hbm.at[rows(turn)], local_ref.at[rows(turn), 0:half]),
            (right_hbm.at[rows(turn)], local_ref.at[rows(turn), half:channels]),
            (gate_hbm.at[rows(turn)], gate_ref.at[rows(turn)]),
        )
        return [
            pltpu.make_async_copy(source, target, sems.at[i, turn])
            for i, (source, target) in enumerate(moves)
        ]

    def leave(turn):
        return pltpu.make_async_copy(out_ref.at[rows(turn)], out_hbm.at[rows(turn)], sems.at[4, turn])

    small = [
        pltpu.make_async_copy(read_hbm, read_ref, sems.at[3, 2]),
        pltpu.make_async_copy(fade_hbm, fade_ref, sems.at[3, 3]),
        pltpu.make_async_copy(rowed_hbm, rowed, sems.at[3, 4]),
    ]
    for copy in small:
        copy.start()
    for turn in range(turns):
        for copy in fetch(turn):
            copy.start()
    ones = head_spread(heads, channels)
    spread[...] = jnp.concatenate([ones, ones], axis=0).astype(BF16)
    for k in range(owners):
        value = decode(state_ref[k, 0:STATE], state_ref[k, STATE : STATE + 1].astype(F32))
        high, low = split(value)
        states[0:STATE, 128 * k : 128 * (k + 1)] = high
        states[STATE : 2 * STATE, 128 * k : 128 * (k + 1)] = low
    for copy in small:
        copy.wait()
    for copy in fetch(0):
        copy.wait()
    pieces = tokens // CHUNK
    row = iota((8, 128), 0)
    for k in range(owners):
        lanes = slice(128 * k, 128 * (k + 1))
        firsts = state_ref[k, STATE : STATE + EXTRA].astype(F32)
        value0, value1, value2 = (firsts[t : t + 1] + firsts[t + 3 : t + 4] for t in (1, 2, 3))
        skip, mix01, mix02, mix12 = (rowed[pieces + i : pieces + i + 1, lanes] for i in range(4))
        patch = jnp.where(row == 2, skip * value2, local_ref[0:8, lanes])
        patch = jnp.where(row == 1, skip * value1 - mix12 * value2, patch)
        patch = jnp.where(row == 0, skip * value0 - mix01 * value1 - mix02 * value2, patch)
        local_ref[0:8, lanes] = patch

    def work(turn):
        span = rows(turn)
        read = read_ref[span]
        both = jnp.concatenate([read, read], axis=1)
        fade = fade_ref[span]
        squares = jnp.zeros((CHUNK, 128), F32)
        for j in range(channels // LANES):
            lanes = slice(LANES * j, LANES * (j + 1))
            reach = dot(both, states[:, lanes]) * dot(fade, spread[:, lanes])
            opened = silu_of_half(gate_ref[span, lanes].astype(F32) * 0.5)
            part = (local_ref[span, lanes] + reach) * opened
            gated[:, lanes] = part
            for i in range(LANES // 128):
                piece = part[:, 128 * i : 128 * (i + 1)]
                squares = squares + piece * piece
        inverse = lax.rsqrt(jnp.sum(squares, axis=1, keepdims=True) * (1.0 / channels) + 1e-05)
        for j in range(channels // LANES):
            lanes = slice(LANES * j, LANES * (j + 1))
            out_ref[span, lanes] = (gated[:, lanes] * inverse * gain_ref[:, lanes]).astype(BF16)
        leave(turn).start()

    work(0)

    def later(turn, carry):
        for copy in fetch(turn):
            copy.wait()
        work(turn)
        return carry

    lax.fori_loop(1, turns, later, 0)
    for turn in range(turns):
        leave(turn).wait()


def final_part(entering, norm_gain, read, fade, rowed, left, right, gate):
    tokens, channels = gate.shape
    heads = channels // HEAD
    hbm = pl.BlockSpec(memory_space=pltpu.HBM)
    vmem = pl.BlockSpec(memory_space=pltpu.VMEM)
    return pl.pallas_call(
        final_kernel,
        in_specs=[vmem] * 2 + [hbm] * 6,
        out_specs=hbm,
        out_shape=pltpu.HBM((tokens, channels), BF16),
        scratch_shapes=[
            pltpu.VMEM(read.shape, BF16),
            pltpu.VMEM(fade.shape, BF16),
            pltpu.VMEM(rowed.shape, F32),
            pltpu.VMEM((tokens, channels), F32),
            pltpu.VMEM(gate.shape, BF16),
            pltpu.VMEM((2 * STATE, channels), BF16),
            pltpu.VMEM((2 * heads, channels), BF16),
            pltpu.VMEM((CHUNK, channels), F32),
            pltpu.VMEM((tokens, channels), BF16),
            pltpu.SemaphoreType.DMA((5, tokens // CHUNK)),
        ],
        compiler_params=pltpu.CompilerParams(vmem_limit_bytes=VMEM_BYTES),
        name="final_part",
    )(entering, norm_gain, *in_hbm(read, fade, rowed, left, right, gate))


def shards(x, weight, gate, write, read, step, decay, skip, norm_gain):
    place = lax.axis_index("ctx")
    turns = x.shape[1] // LANES
    ends, value = end_state(x, weight, write, step, decay)
    received = lax.all_to_all(ends, "ctx", 0, 0)
    decay, ends = lax.optimization_barrier((decay, ends))
    gains, fades, reach, keys, mix, rowed = local_tables(write, read, step, decay, skip[:, None])
    part = turns // 4
    left = local_part(0, part, value, gains, fades, keys, mix, rowed)
    received, left = lax.optimization_barrier((received, left))
    entering = prefix(place[None], received, weight)
    value, entering = lax.optimization_barrier((value, entering))
    entering = lax.all_to_all(entering, "ctx", 0, 0)
    right = local_part(part, turns - part, value, gains, fades, keys, mix, rowed)
    return final_part(entering, norm_gain[None, :], read, reach, rowed, left, right, gate)


def solution(mesh):
    placed = (
        P("ctx", "tp"),
        P(None, "tp"),
        P("ctx", "tp"),
        P("ctx", "tp"),
        P("ctx", "tp"),
        P("tp", "ctx"),
        P("tp", "ctx"),
        P("tp"),
        P("tp"),
    )
    return jax.shard_map(
        shards, mesh=mesh, in_specs=placed, out_specs=P("ctx", "tp"), check_vma=False
    )
```

time: 820 us -> 58.6 us (0.07)
  the two profiles are of different devices: /device:TPU:22 before, /device:TPU:0 now
where the time goes in v2:
time: 58.6 us; the launch traced here: 58.1 us
  Pallas kernels  42.2 us (72%)
  starting transfers between devices  13.5 us (23%)
  waiting for transfers between devices  2 us (3%)
    pallas_call x2, Pallas kernels, local_part(): pl.pallas_call(functools.partial(local_kernel, begin), in_specs=[hbm] * 6...  17.7 us
    pallas_call x1, Pallas kernels, end_state(): pl.pallas_call(end_state_kernel, in_specs=[pl.BlockSpec(memory_space=pltp...  10.8 us
    pallas_call x1, Pallas kernels, final_part(): pl.pallas_call(final_kernel, in_specs=[vmem] * 2 + [hbm] * 6, out_specs=h...  8.19 us
    all_to_all x1, starting transfers between devices, shards(): received = lax.all_to_all(ends, 'ctx', 0, 0)  8.14 us
    all_to_all x1, starting transfers between devices, shards(): entering = lax.all_to_all(entering, 'ctx', 0, 0)  5.31 us
    pallas_call x1, Pallas kernels, local_tables(): pl.pallas_call(local_tables_kernel, in_specs=[hbm] * 4 + [pl.BlockSpec(me...  3.69 us
    all_to_all x1, waiting for transfers between devices, shards(): received = lax.all_to_all(ends, 'ctx', 0, 0)  1.93 us
    pallas_call x1, Pallas kernels, prefix(): pl.pallas_call(prefix_kernel, in_specs=[pl.BlockSpec(memory_space=pltpu.S...  1.91 us
  transfers between devices with their start and end apart: 2, of which 2 were waited for; matrix products, arithmetic and copies ran while one was open for 0% of the time, Pallas kernels for 37%

profile of v2, /device:TPU:0, one launch (start us, length us, event | category | flops | bytes accessed | tf_op | source)
XLA Modules:
  0.0 58.1 jit_solution(1222202953574563455)
XLA Ops:
  0.0 0.0 copy-start.2
  0.0 10.8 %end_state.1 = (bf16[16,144,128]{2,1,0:T(8,128)(2,1)}, f32[1024,2048]{1,0:T(8,128)}) custom-call(bf16[1024,2048]{1,0:T(8,128)(2,1)} %x_hbm.1, f32[4,2048]{1,0:T(4,128)} %weight_ref.1, bf16[1024,128]{1,0:T(8,128)(2,1)} %write_hbm.3, f32[32,1024]{1,0:T(8,128)} %step_hbm.3, f32[32,1024]{1,0:T(8,128)} %decay_hbm.2), custom_call_target="tpu_custom_call" | custom-call | tf_op jit(solution)/shard_map/end_state/pallas_call | solution.py:229
  10.8 8.1 %all-to-all-start = ((bf16[16,144,128]{2,1,0:T(8,128)(2,1)}), bf16[16,144,128]{2,1,0:T(8,128)(2,1)S(1)}, u32[]{:S(2)}, u32[]{:S(2)}) async-start(bf16[16,144,128]{2,1,0:T(8,128)(2,1)} %get-tuple-element.19), calls=%async_computation | async-start | bytes 1179648 | tf_op jit(solution)/shard_map/all_to_all | solution.py:645
  18.9 0.0 copy-done.2
  19.0 0.1 copy.10.skip_ref
  19.0 3.7 %local_tables.1 = (bf16[1024,64]{1,0:T(8,128)(2,1)}, bf16[1024,64]{1,0:T(8,128)(2,1)}, bf16[1024,64]{1,0:T(8,128)(2,1)}, bf16[1024,256]{1,0:T(8,128)(2,1)}, bf16...) custom-call(bf16[1024,128]{1,0:T(8,128)(2,1)} %write_hbm.3, bf16[1024,128]{1,0:T(8,128)(2,1)} %read_hbm.3, f32[32,1024]{1,0:T(8,128)} %step_hbm.3, ...), custom_call_target="tpu_custom_call" | custom-call | tf_op jit(solution)/shard_map/local_tables/pallas_call | solution.py:398
  22.7 0.0 copy-start
  22.8 6.1 %local_part.2.left_hbm = f32[1024,512]{1,0:T(8,128)} custom-call(f32[1024,2048]{1,0:T(8,128)} %get-tuple-element.30.value_hbm, bf16[1024,64]{1,0:T(8,128)(2,1)} %get-tuple-element.21.gains_hbm, bf16[1024,64]{1,0:T(8,128)(2,1)} %get-tuple-element.22.fades_hbm, bf16[1024,256]{1,0:T(8,128)(2,1)} %get-tuple-element.23.keys_hbm, ...), custom_call_target="tpu_custom_call" | custom-call | tf_op jit(solution)/shard_map/local_part/pallas_call | solution.py:494
  28.9 1.9 %all-to-all-done.in_ref = bf16[16,144,128]{2,1,0:T(8,128)(2,1)S(1)} async-done(((bf16[16,144,128]{2,1,0:T(8,128)(2,1)}), bf16[16,144,128]{2,1,0:T(8,128)(2,1)S(1)}, u32[]{:S(2)}, u32[]{:S(2)}) %all-to-all-start) | async-done | bytes 589856 | tf_op jit(solution)/shard_map/all_to_all | solution.py:645
  30.8 0.0 copy-done
  30.8 1.9 %prefix.1 = bf16[16,144,128]{2,1,0:T(8,128)(2,1)} custom-call(s32[1]{0:T(128)} %bitcast.place_ref, bf16[16,144,128]{2,1,0:T(8,128)(2,1)S(1)} %all-to-all-done.in_ref, f32[4,2048]{1,0:T(4,128)S(1)} %copy-done), custom_call_target="tpu_custom_call" | custom-call | tf_op jit(solution)/shard_map/prefix/pallas_call | solution.py:305
  32.8 5.3 %all-to-all-start.1 = ((bf16[16,144,128]{2,1,0:T(8,128)(2,1)}), bf16[16,144,128]{2,1,0:T(8,128)(2,1)S(1)}, u32[]{:S(2)}, u32[]{:S(2)}) async-start(bf16[16,144,128]{2,1,0:T(8,128)(2,1)} %prefix.1), calls=%async_computation.1 | async-start | bytes 1179648 | tf_op jit(solution)/shard_map/all_to_all | solution.py:653
  38.1 0.0 copy-start.1
  38.1 11.5 %local_part.3.right_hbm = f32[1024,1536]{1,0:T(8,128)} custom-call(f32[1024,2048]{1,0:T(8,128)} %get-tuple-element.30.value_hbm, bf16[1024,64]{1,0:T(8,128)(2,1)} %get-tuple-element.21.gains_hbm, bf16[1024,64]{1,0:T(8,128)(2,1)} %get-tuple-element.22.fades_hbm, bf16[1024,256]{1,0:T(8,128)(2,1)} %get-tuple-element.23.keys_hbm, ...), custom_call_target="tpu_custom_call" | custom-call | tf_op jit(solution)/shard_map/local_part/pallas_call | solution.py:494
  49.6 0.1 all-to-all-done.1.state_ref
  49.7 0.0 copy-done.1
  49.7 8.2 %final_part.1 = bf16[1024,2048]{1,0:T(8,128)(2,1)} custom-call(bf16[16,144,128]{2,1,0:T(8,128)(2,1)S(1)} %all-to-all-done.1.state_ref, f32[1,2048]{1,0:T(1,128)S(1)} %bitcast.3, bf16[1024,128]{1,0:T(8,128)(2,1)} %read_hbm.3, bf16[1024,64]{1,0:T(8,128)(2,1)} %get-tuple-element.28.fade_hbm, f32[16,2048]{1,0:T(8,128)} %get-tuple-element.25.rowed_hbm, ...), custom_call_target="tpu_custom_call" | custom-call | tf_op jit(solution)/shard_map/final_part/pallas_call | solution.py:619
Async XLA Ops:
  0.0 19.0 %copy-start.2 = (f32[32]{0:T(128)S(1)}, f32[32]{0:T(128)}, u32[]{:S(2)}) copy-start(f32[32]{0:T(128)} %param.16) | copy-start | bytes 388
  10.8 20.0 %all-to-all-start = ((bf16[16,144,128]{2,1,0:T(8,128)(2,1)}), bf16[16,144,128]{2,1,0:T(8,128)(2,1)S(1)}, u32[]{:S(2)}, u32[]{:S(2)}) async-start(bf16[16,144,128]{2,1,0:T(8,128)(2,1)} %get-tuple-element.19), calls=%async_computation | async-start | bytes 1179648 | tf_op jit(solution)/shard_map/all_to_all | solution.py:645
  22.7 8.1 %copy-start = (f32[4,2048]{1,0:T(4,128)S(1)}, f32[4,2048]{1,0:T(4,128)}, u32[]{:S(2)}) copy-start(f32[4,2048]{1,0:T(4,128)} %weight_ref.1) | copy-start | bytes 98308
  32.8 16.9 %all-to-all-start.1 = ((bf16[16,144,128]{2,1,0:T(8,128)(2,1)}), bf16[16,144,128]{2,1,0:T(8,128)(2,1)S(1)}, u32[]{:S(2)}, u32[]{:S(2)}) async-start(bf16[16,144,128]{2,1,0:T(8,128)(2,1)} %prefix.1), calls=%async_computation.1 | async-start | bytes 1179648 | tf_op jit(solution)/shard_map/all_to_all | solution.py:653
  38.1 11.6 %copy-start.1 = (f32[2048]{0:T(1024)S(1)}, f32[2048]{0:T(1024)}, u32[]{:S(2)}) copy-start(f32[2048]{0:T(1024)} %param.17) | copy-start | bytes 24580

commit v3 on v2

--- a/solution.py
+++ b/solution.py
@@ -15,7 +15,6 @@
 CHUNK = 128
 LANES = 256
 EXTRA = 16
-HIGHEST = lax.Precision.HIGHEST
 VMEM_BYTES = 24 * 1024 * 1024
 
 
@@ -27,8 +26,13 @@
     return jnp.dot(a, b, preferred_element_type=F32)
 
 
-def dot_exact(a, b):
-    return jnp.dot(a, b, preferred_element_type=F32, precision=HIGHEST)
+def dot_binary(a, b):
+    high = a.astype(BF16)
+    rest = a - high.astype(F32)
+    middle = rest.astype(BF16)
+    low = (rest - middle.astype(F32)).astype(BF16)
+    b = b.astype(BF16)
+    return dot(jnp.concatenate([high, middle, low], axis=1), jnp.concatenate([b, b, b], axis=0))
 
 
 def split(value):
@@ -43,14 +47,11 @@
 def encode(value):
     top = jnp.max(jnp.abs(value), axis=0, keepdims=True)
     scale = jnp.maximum(top * 1.00390625, 1e-30).astype(BF16).astype(F32)
-    size = jnp.exp2(jnp.abs(value) * (252.0 / scale) - 126.0)
-    return jnp.where(value < 0, -size, size).astype(BF16), scale
+    return jnp.exp2(value * (126.0 / scale)).astype(BF16), scale
 
 
 def decode(code, scale):
-    code = code.astype(F32)
-    size = (jnp.log2(jnp.abs(code)) + 126.0) * (scale * (1.0 / 252.0))
-    return jnp.where(code < 0, -size, size)
+    return jnp.log2(code.astype(F32)) * (scale * (1.0 / 126.0))
 
 
 def stack_chunks(value):
@@ -127,7 +128,7 @@
     decay = decay_ref[...]
     logs = stack_chunks(decay)
     later = (iota((CHUNK, CHUNK), 0) > iota((CHUNK, CHUNK), 1)).astype(F32)
-    suffix = dot_exact(logs, later)
+    suffix = dot_binary(logs, later)
     total = suffix[:, 0:1] + logs[:, 0:1]
     offset = jnp.zeros((heads, 1), F32)
     offsets = []
@@ -148,7 +149,7 @@
     scalars = jnp.where(lane == 0, jnp.exp(offset), 0.0)
     for t, run in enumerate((run0, run1, run2)):
         scalars = jnp.where(lane == t + 1, jnp.exp(-run) * step[:, t : t + 1], scalars)
-    wide = dot_exact(scalars.T[0:8], ones)
+    wide = dot_binary(scalars.T[0:8], ones)
     segment = (iota(wide.shape, 1) % HEAD) // (HEAD // 4)
     packed[...] = jnp.broadcast_to(
         jnp.sum(jnp.where(iota(wide.shape, 0) == segment, wide, 0.0), axis=0, keepdims=True),
@@ -156,7 +157,7 @@
     )
     small[2].wait()
     small[3].wait()
-    write_t = write_ref[...].astype(F32).T.astype(BF16)
+    write_t = write_ref[...].T
     for c in range(pieces):
         part = write_t[:, CHUNK * c : CHUNK * (c + 1)]
         keys[CHUNK * c : CHUNK * (c + 1)] = jnp.concatenate([part, part], axis=1)
@@ -313,31 +314,16 @@
     )(place, received, weight)
 
 
-def local_tables_kernel(
-    write_hbm, read_hbm, step_hbm, decay_hbm, skip_ref, gains_out, fades_out, reach_out, keys_out, mix_out, rowed_out,
-    write_ref, read_ref, step_ref, decay_ref, gains, fades, reach, keys, mix, rowed, sems,
+def make_tables(
+    write_ref, read_ref, step_ref, decay_ref, skip_ref, gains, fades, reach, keys, mix, rowed
 ):
     heads, tokens = step_ref.shape
     pieces = tokens // CHUNK
     channels = heads * HEAD
-    moves = [
-        pltpu.make_async_copy(source, target, sems.at[i])
-        for i, (source, target) in enumerate(
-            (
-                (decay_hbm, decay_ref), (step_hbm, step_ref), (write_hbm, write_ref), (read_hbm, read_ref),
-                (gains, gains_out), (fades, fades_out), (reach, reach_out), (keys, keys_out), (mix, mix_out),
-                (rowed, rowed_out),
-            )
-        )
-    ]
-    for copy in moves[:4]:
-        copy.start()
     ones = head_spread(heads, channels)
-    for copy in moves[:4]:
-        copy.wait()
     logs = stack_chunks(decay_ref[...])
     upto = (iota((CHUNK, CHUNK), 0) <= iota((CHUNK, CHUNK), 1)).astype(F32)
-    run = dot_exact(logs, upto)
+    run = dot_binary(logs, upto)
     middle = run[:, CHUNK // 2 - 1 : CHUNK // 2]
     total = run[:, CHUNK - 1 : CHUNK]
     gain = jnp.exp(middle - run) * stack_chunks(step_ref[...])
@@ -374,56 +360,18 @@
         mix[span] = jnp.concatenate([high, high, low, read, read], axis=1)
         write_t = write.astype(F32).T.astype(BF16)
         keys[span] = jnp.concatenate([write_t, write_t], axis=1)
-    rowed[...] = dot_exact(scalars.T[0 : rowed.shape[0]], ones)
-    for copy in moves[4:]:
-        copy.start()
-    for copy in moves[4:]:
-        copy.wait()
-
-
-def local_tables(write, read, step, decay, skip):
-    heads, tokens = step.shape
-    pieces = tokens // CHUNK
-    channels = heads * HEAD
-    hbm = pl.BlockSpec(memory_space=pltpu.HBM)
-    outs = [
-        ((tokens, 2 * heads), BF16),
-        ((tokens, 2 * heads), BF16),
-        ((tokens, 2 * heads), BF16),
-        ((tokens, 2 * CHUNK), BF16),
-        ((tokens, 5 * CHUNK), BF16),
-        ((pieces + 8, channels), F32),
-    ]
-    ins = (write, read, step, decay)
-    return pl.pallas_call(
-        local_tables_kernel,
-        in_specs=[hbm] * 4 + [pl.BlockSpec(memory_space=pltpu.VMEM)],
-        out_specs=[hbm] * len(outs),
-        out_shape=[pltpu.HBM(*out) for out in outs],
-        scratch_shapes=[pltpu.VMEM(value.shape, value.dtype) for value in ins]
-        + [pltpu.VMEM(*out) for out in outs]
-        + [pltpu.SemaphoreType.DMA((len(ins) + len(outs),))],
-        compiler_params=pltpu.CompilerParams(vmem_limit_bytes=VMEM_BYTES),
-        name="local_tables",
-    )(*in_hbm(*ins), skip)
-
-
-def local_kernel(
-    begin, value_hbm, gains_hbm, fades_hbm, keys_hbm, mix_hbm, rowed_hbm, local_hbm,
-    value_ref, gains, fades, keys, mix, rowed, spread, gain0, gain1, fade0, fade1, result, sems,
+    rowed[...] = dot_binary(scalars.T[0 : rowed.shape[0]], ones)
+
+
+def local_slices(
+    begin, ready, value_hbm, local_hbm, gains, fades, keys, mix, rowed,
+    value_ref, spread, gain0, gain1, fade0, fade1, result, sems,
 ):
     tokens, width = local_hbm.shape
     pieces = tokens // CHUNK
     channels = rowed.shape[1]
     turns = width // LANES
     wide_gains, wide_fades = (gain0, gain1), (fade0, fade1)
-    pairs = (
-        (gains_hbm, gains), (keys_hbm, keys), (mix_hbm, mix), (rowed_hbm, rowed), (fades_hbm, fades)
-    )
-    small = [
-        pltpu.make_async_copy(source, target, sems.at[2 * turns + i])
-        for i, (source, target) in enumerate(pairs)
-    ]
 
     def columns(turn):
         return pl.ds(pl.multiple_of(turn * LANES, LANES), LANES)
@@ -443,16 +391,11 @@
         wide_gains[side][...] = dot(gains[...], spread[:, lanes])
         wide_fades[side][...] = dot(fades[...], spread[:, lanes])
 
-    small[0].start()
-    fetch(0).start()
-    for copy in small[1:]:
-        copy.start()
-    for turn in range(1, turns):
+    for turn in range(turns):
         fetch(turn).start()
     ones = head_spread(channels // HEAD, channels)
     spread[...] = jnp.concatenate([ones, ones], axis=0).astype(BF16)
-    for copy in small:
-        copy.wait()
+    ready()
     widen(0, 0)
 
     def work(turn, side):
@@ -487,33 +430,115 @@
         leave(turn).wait()
 
 
-def local_part(begin, turns, value, gains, fades, keys, mix, rowed):
+def first_kernel(
+    begin, write_hbm, read_hbm, step_hbm, decay_hbm, skip_ref, value_hbm, *refs
+):
+    outs, local_hbm, ins, tables, rest = refs[0:6], refs[6], refs[7:11], refs[11:17], refs[17:-1]
+    sems = refs[-1]
+    arrive = [
+        pltpu.make_async_copy(source, target, sems.at[i])
+        for i, (source, target) in enumerate(
+            zip((write_hbm, read_hbm, step_hbm, decay_hbm), ins, strict=True)
+        )
+    ]
+    depart = [
+        pltpu.make_async_copy(source, target, sems.at[4 + i])
+        for i, (source, target) in enumerate(zip(tables, outs, strict=True))
+    ]
+    for copy in arrive:
+        copy.start()
+
+    def ready():
+        for copy in arrive:
+            copy.wait()
+        make_tables(*ins, skip_ref, *tables)
+        for copy in depart:
+            copy.start()
+
+    gains, fades, _, keys, mix, rowed = tables
+    local_slices(begin, ready, value_hbm, local_hbm, gains, fades, keys, mix, rowed, *rest)
+    for copy in depart:
+        copy.wait()
+
+
+def second_kernel(
+    begin, gains_hbm, fades_hbm, keys_hbm, mix_hbm, rowed_hbm, value_hbm, local_hbm, *refs
+):
+    tables, rest, sems = refs[0:5], refs[5:-1], refs[-1]
+    arrive = [
+        pltpu.make_async_copy(source, target, sems.at[i])
+        for i, (source, target) in enumerate(
+            zip((gains_hbm, fades_hbm, keys_hbm, mix_hbm, rowed_hbm), tables, strict=True)
+        )
+    ]
+    for copy in arrive:
+        copy.start()
+
+    def ready():
+        for copy in arrive:
+            copy.wait()
+
+    local_slices(begin, ready, value_hbm, local_hbm, *tables, *rest)
+
+
+def slice_scratch(turns, tokens, channels):
+    return [
+        pltpu.VMEM((turns, tokens, LANES), F32),
+        pltpu.VMEM((2 * (channels // HEAD), channels), BF16),
+        pltpu.VMEM((tokens, LANES), F32),
+        pltpu.VMEM((tokens, LANES), F32),
+        pltpu.VMEM((tokens, LANES), F32),
+        pltpu.VMEM((tokens, LANES), F32),
+        pltpu.VMEM((turns, tokens, LANES), F32),
+        pltpu.SemaphoreType.DMA((2 * turns,)),
+    ]
+
+
+def first_local(turns, write, read, step, decay, skip, value):
+    heads, tokens = step.shape
+    pieces = tokens // CHUNK
+    channels = heads * HEAD
+    hbm = pl.BlockSpec(memory_space=pltpu.HBM)
+    tables = [
+        ((tokens, 2 * heads), BF16),
+        ((tokens, 2 * heads), BF16),
+        ((tokens, 2 * heads), BF16),
+        ((tokens, 2 * CHUNK), BF16),
+        ((tokens, 5 * CHUNK), BF16),
+        ((pieces + 8, channels), F32),
+    ]
+    ins = (write, read, step, decay)
+    *out, local = pl.pallas_call(
+        functools.partial(first_kernel, 0),
+        in_specs=[hbm] * 4 + [pl.BlockSpec(memory_space=pltpu.VMEM), hbm],
+        out_specs=[hbm] * 7,
+        out_shape=[pltpu.HBM(*table) for table in tables]
+        + [pltpu.HBM((tokens, turns * LANES), F32)],
+        scratch_shapes=[pltpu.VMEM(source.shape, source.dtype) for source in ins]
+        + [pltpu.VMEM(*table) for table in tables]
+        + slice_scratch(turns, tokens, channels)
+        + [pltpu.SemaphoreType.DMA((len(ins) + len(tables),))],
+        compiler_params=pltpu.CompilerParams(vmem_limit_bytes=VMEM_BYTES),
+        name="first_local",
+    )(*in_hbm(*ins), skip, *in_hbm(value))
+    return out, local
+
+
+def second_local(begin, turns, gains, fades, keys, mix, rowed, value):
     tokens, channels = value.shape
     hbm = pl.BlockSpec(memory_space=pltpu.HBM)
-    inputs = in_hbm(value, gains, fades, keys, mix, rowed)
+    tables = (gains, fades, keys, mix, rowed)
     return pl.pallas_call(
-        functools.partial(local_kernel, begin),
+        functools.partial(second_kernel, begin),
         in_specs=[hbm] * 6,
         out_specs=hbm,
         out_shape=pltpu.HBM((tokens, turns * LANES), F32),
-        scratch_shapes=[
-            pltpu.VMEM((turns, tokens, LANES), F32),
-            pltpu.VMEM(gains.shape, BF16),
-            pltpu.VMEM(fades.shape, BF16),
-            pltpu.VMEM(keys.shape, BF16),
-            pltpu.VMEM(mix.shape, BF16),
-            pltpu.VMEM(rowed.shape, F32),
-            pltpu.VMEM((2 * (channels // HEAD), channels), BF16),
-            pltpu.VMEM((tokens, LANES), F32),
-            pltpu.VMEM((tokens, LANES), F32),
-            pltpu.VMEM((tokens, LANES), F32),
-            pltpu.VMEM((tokens, LANES), F32),
-            pltpu.VMEM((turns, tokens, LANES), F32),
-            pltpu.SemaphoreType.DMA((2 * turns + 5,)),
-        ],
+        scratch_shapes=[pltpu.VMEM(table.shape, table.dtype) for table in tables]
+        + slice_scratch(turns, tokens, channels)
+        + [pltpu.SemaphoreType.DMA((len(tables),))],
         compiler_params=pltpu.CompilerParams(vmem_limit_bytes=VMEM_BYTES),
-        name="local_part",
-    )(*inputs)
+        name="second_local",
+    )(*in_hbm(*tables, value))
 
 
 def final_kernel(
@@ -586,7 +611,7 @@
         for j in range(channels // LANES):
             lanes = slice(LANES * j, LANES * (j + 1))
             reach = dot(both, states[:, lanes]) * dot(fade, spread[:, lanes])
-            opened = silu_of_half(gate_ref[span, lanes].astype(F32) * 0.5)
+            opened = silu_of_half((gate_ref[span, lanes] * 0.5).astype(F32))
             part = (local_ref[span, lanes] + reach) * opened
             gated[:, lanes] = part
             for i in range(LANES // 128):
@@ -644,14 +669,14 @@
     ends, value = end_state(x, weight, write, step, decay)
     received = lax.all_to_all(ends, "ctx", 0, 0)
     decay, ends = lax.optimization_barrier((decay, ends))
-    gains, fades, reach, keys, mix, rowed = local_tables(write, read, step, decay, skip[:, None])
-    part = turns // 4
-    left = local_part(0, part, value, gains, fades, keys, mix, rowed)
+    part = turns // 2
+    tables, left = first_local(part, write, read, step, decay, skip[:, None], value)
+    gains, fades, reach, keys, mix, rowed = tables
     received, left = lax.optimization_barrier((received, left))
     entering = prefix(place[None], received, weight)
     value, entering = lax.optimization_barrier((value, entering))
     entering = lax.all_to_all(entering, "ctx", 0, 0)
-    right = local_part(part, turns - part, value, gains, fades, keys, mix, rowed)
+    right = second_local(part, turns - part, gains, fades, keys, mix, rowed, value)
     return final_part(entering, norm_gain[None, :], read, reach, rowed, left, right, gate)
 
 

time: 58.6 us -> 57 us (0.973)
  Pallas kernels: 42.2 us -> 39 us
  waiting for transfers between devices: 2 us -> 4.11 us
    all_to_all x1, waiting for transfers between devices: 0.07 us -> 2.18 us  [shards(): entering = lax.all_to_all(entering, 'ctx', 0, 0)]
    pallas_call x3 -> x2, Pallas kernels: 21.4 us -> 19.3 us  [the longest x1 9.85 us: first_local(): pl.pallas_call(functools.partial(first_kernel, 0), in_specs=[hbm] * 4 + [...]
  transfers between devices with their start and end apart: 2 -> 2, of which waited for: 2 -> 2; matrix products, arithmetic and copies ran while one was open for 0% -> 0% of each run, Pallas kernels for 37% -> 34%
where the time goes in v3:
time: 57 us; the launch traced here: 56.7 us
  Pallas kernels  39 us (68%)
  starting transfers between devices  13.4 us (24%)
  waiting for transfers between devices  4.11 us (7%)
    pallas_call x1, Pallas kernels, end_state(): pl.pallas_call(end_state_kernel, in_specs=[pl.BlockSpec(memory_space=pltp...  10.5 us
    pallas_call x1, Pallas kernels, first_local(): pl.pallas_call(functools.partial(first_kernel, 0), in_specs=[hbm] * 4 + [...  9.85 us
    pallas_call x1, Pallas kernels, second_local(): pl.pallas_call(functools.partial(second_kernel, begin), in_specs=[hbm] *...  9.44 us
    all_to_all x1, starting transfers between devices, shards(): received = lax.all_to_all(ends, 'ctx', 0, 0)  8.14 us
    pallas_call x1, Pallas kernels, final_part(): pl.pallas_call(final_kernel, in_specs=[vmem] * 2 + [hbm] * 6, out_specs=h...  7.69 us
    all_to_all x1, starting transfers between devices, shards(): entering = lax.all_to_all(entering, 'ctx', 0, 0)  5.3 us
    all_to_all x1, waiting for transfers between devices, shards(): entering = lax.all_to_all(entering, 'ctx', 0, 0)  2.18 us
    all_to_all x1, waiting for transfers between devices, shards(): received = lax.all_to_all(ends, 'ctx', 0, 0)  1.93 us
  transfers between devices with their start and end apart: 2, of which 2 were waited for; matrix products, arithmetic and copies ran while one was open for 0% of the time, Pallas kernels for 34%

profile of v3, /device:TPU:0, one launch (start us, length us, event | category | flops | bytes accessed | tf_op | source)
XLA Modules:
  0.0 56.7 jit_solution(1754822678661451723)
XLA Ops:
  0.0 0.0 copy-start.2
  0.0 10.5 %end_state.1 = (bf16[16,144,128]{2,1,0:T(8,128)(2,1)}, f32[1024,2048]{1,0:T(8,128)}) custom-call(bf16[1024,2048]{1,0:T(8,128)(2,1)} %x_hbm.1, f32[4,2048]{1,0:T(4,128)} %weight_ref.1, bf16[1024,128]{1,0:T(8,128)(2,1)} %write_hbm.3, f32[32,1024]{1,0:T(8,128)} %step_hbm.3, f32[32,1024]{1,0:T(8,128)} %decay_hbm.2), custom_call_target="tpu_custom_call" | custom-call | tf_op jit(solution)/shard_map/end_state/pallas_call | solution.py:230
  10.5 8.1 %all-to-all-start = ((bf16[16,144,128]{2,1,0:T(8,128)(2,1)}), bf16[16,144,128]{2,1,0:T(8,128)(2,1)S(1)}, u32[]{:S(2)}, u32[]{:S(2)}) async-start(bf16[16,144,128]{2,1,0:T(8,128)(2,1)} %get-tuple-element.20), calls=%async_computation | async-start | bytes 1179648 | tf_op jit(solution)/shard_map/all_to_all | solution.py:670
  18.6 0.0 copy-done.2
  18.6 0.1 copy.10.skip_ref
  18.7 0.0 copy-start
  18.7 9.9 %first_local.1 = (bf16[1024,64]{1,0:T(8,128)(2,1)}, bf16[1024,64]{1,0:T(8,128)(2,1)}, bf16[1024,64]{1,0:T(8,128)(2,1)}, bf16[1024,256]{1,0:T(8,128)(2,1)}, bf16[...) custom-call(bf16[1024,128]{1,0:T(8,128)(2,1)} %write_hbm.3, bf16[1024,128]{1,0:T(8,128)(2,1)} %read_hbm.3, ...), custom_call_target="tpu_custom_call" | custom-call | tf_op jit(solution)/shard_map/first_local/pallas_call | solution.py:511
  28.6 1.9 %all-to-all-done.in_ref = bf16[16,144,128]{2,1,0:T(8,128)(2,1)S(1)} async-done(((bf16[16,144,128]{2,1,0:T(8,128)(2,1)}), bf16[16,144,128]{2,1,0:T(8,128)(2,1)S(1)}, u32[]{:S(2)}, u32[]{:S(2)}) %all-to-all-start) | async-done | bytes 589856 | tf_op jit(solution)/shard_map/all_to_all | solution.py:670
  30.5 0.0 copy-done
  30.5 1.5 %prefix.1 = bf16[16,144,128]{2,1,0:T(8,128)(2,1)} custom-call(s32[1]{0:T(128)} %bitcast.place_ref, bf16[16,144,128]{2,1,0:T(8,128)(2,1)S(1)} %all-to-all-done.in_ref, f32[4,2048]{1,0:T(4,128)S(1)} %copy-done), custom_call_target="tpu_custom_call" | custom-call | tf_op jit(solution)/shard_map/prefix/pallas_call | solution.py:306
  32.1 5.3 %all-to-all-start.1 = ((bf16[16,144,128]{2,1,0:T(8,128)(2,1)}), bf16[16,144,128]{2,1,0:T(8,128)(2,1)S(1)}, u32[]{:S(2)}, u32[]{:S(2)}) async-start(bf16[16,144,128]{2,1,0:T(8,128)(2,1)} %prefix.1), calls=%async_computation.1 | async-start | bytes 1179648 | tf_op jit(solution)/shard_map/all_to_all | solution.py:678
  37.4 0.0 copy-start.1
  37.4 9.4 %second_local.1.right_hbm = f32[1024,1024]{1,0:T(8,128)} custom-call(bf16[1024,64]{1,0:T(8,128)(2,1)} %get-tuple-element.28.gains_hbm, bf16[1024,64]{1,0:T(8,128)(2,1)} %get-tuple-element.29.fades_hbm, bf16[1024,256]{1,0:T(8,128)(2,1)} %get-tuple-element.30.keys_hbm, bf16[1024,640]{1,0:T(8,128)(2,1)} %get-tuple-element.31.mix_hbm, ...), custom_call_target="tpu_custom_call" | custom-call | tf_op jit(solution)/shard_map/second_local/pallas_call | solution.py:531
  46.8 2.2 %all-to-all-done.1.state_ref = bf16[16,144,128]{2,1,0:T(8,128)(2,1)S(1)} async-done(((bf16[16,144,128]{2,1,0:T(8,128)(2,1)}), bf16[16,144,128]{2,1,0:T(8,128)(2,1)S(1)}, u32[]{:S(2)}, u32[]{:S(2)}) %all-to-all-start.1) | async-done | bytes 589856 | tf_op jit(solution)/shard_map/all_to_all | solution.py:678
  49.0 0.0 copy-done.1
  49.0 7.7 %final_part.1 = bf16[1024,2048]{1,0:T(8,128)(2,1)} custom-call(bf16[16,144,128]{2,1,0:T(8,128)(2,1)S(1)} %all-to-all-done.1.state_ref, f32[1,2048]{1,0:T(1,128)S(1)} %bitcast.3, bf16[1024,128]{1,0:T(8,128)(2,1)} %read_hbm.3, bf16[1024,64]{1,0:T(8,128)(2,1)} %get-tuple-element.25.fade_hbm, f32[16,2048]{1,0:T(8,128)} %get-tuple-element.26.rowed_hbm, ...), custom_call_target="tpu_custom_call" | custom-call | tf_op jit(solution)/shard_map/final_part/pallas_call | solution.py:644
Async XLA Ops:
  0.0 18.6 %copy-start.2 = (f32[32]{0:T(128)S(1)}, f32[32]{0:T(128)}, u32[]{:S(2)}) copy-start(f32[32]{0:T(128)} %param.16) | copy-start | bytes 388
  10.5 20.1 %all-to-all-start = ((bf16[16,144,128]{2,1,0:T(8,128)(2,1)}), bf16[16,144,128]{2,1,0:T(8,128)(2,1)S(1)}, u32[]{:S(2)}, u32[]{:S(2)}) async-start(bf16[16,144,128]{2,1,0:T(8,128)(2,1)} %get-tuple-element.20), calls=%async_computation | async-start | bytes 1179648 | tf_op jit(solution)/shard_map/all_to_all | solution.py:670
  18.7 11.8 %copy-start = (f32[4,2048]{1,0:T(4,128)S(1)}, f32[4,2048]{1,0:T(4,128)}, u32[]{:S(2)}) copy-start(f32[4,2048]{1,0:T(4,128)} %weight_ref.1) | copy-start | bytes 98308
  32.1 16.9 %all-to-all-start.1 = ((bf16[16,144,128]{2,1,0:T(8,128)(2,1)}), bf16[16,144,128]{2,1,0:T(8,128)(2,1)S(1)}, u32[]{:S(2)}, u32[]{:S(2)}) async-start(bf16[16,144,128]{2,1,0:T(8,128)(2,1)} %prefix.1), calls=%async_computation.1 | async-start | bytes 1179648 | tf_op jit(solution)/shard_map/all_to_all | solution.py:678
  37.4 11.6 %copy-start.1 = (f32[2048]{0:T(1024)S(1)}, f32[2048]{0:T(1024)}, u32[]{:S(2)}) copy-start(f32[2048]{0:T(1024)} %param.17) | copy-start | bytes 24580

commit v4 on v3

--- a/solution.py
+++ b/solution.py
@@ -167,6 +167,7 @@
         fetch(turn).wait()
         weight = weight_ref[:, lanes] * 0.5
         state = jnp.zeros((STATE, LANES), F32)
+        held = []
         for c in range(pieces):
             span = slice(CHUNK * c, CHUNK * (c + 1))
             rows = x_ref[span, lanes].astype(F32)
@@ -178,7 +179,12 @@
                 value = conv_silu(stage, part, CHUNK * c, CHUNK, weight[:, cols])
                 value_ref[turn, span, cols] = value
                 sides.append(jnp.concatenate(split(value * gain[:, cols]), axis=0))
-            state = state + dot(keys[span], jnp.concatenate(sides, axis=1))
+            held.append((keys[span], jnp.concatenate(sides, axis=1)))
+            if len(held) == 2:
+                left, right = zip(*held, strict=True)
+                part = dot(jnp.concatenate(left, axis=1), jnp.concatenate(right, axis=0))
+                state = part if c < 2 else state + part
+                held = []
         leave(turn).start()
         return state
 

time: 57 us -> 56.8 us (level)
  no operation moved by 1% of the time
where the time goes in v4:
time: 56.8 us; the launch traced here: 56.5 us
  Pallas kernels  38.8 us (68%)
  starting transfers between devices  13.4 us (24%)
  waiting for transfers between devices  4.1 us (7%)
    pallas_call x1, Pallas kernels, end_state(): pl.pallas_call(end_state_kernel, in_specs=[pl.BlockSpec(memory_space=pltp...  10.3 us
    pallas_call x1, Pallas kernels, first_local(): pl.pallas_call(functools.partial(first_kernel, 0), in_specs=[hbm] * 4 + [...  9.86 us
    pallas_call x1, Pallas kernels, second_local(): pl.pallas_call(functools.partial(second_kernel, begin), in_specs=[hbm] *...  9.44 us
    all_to_all x1, starting transfers between devices, shards(): received = lax.all_to_all(ends, 'ctx', 0, 0)  8.13 us
    pallas_call x1, Pallas kernels, final_part(): pl.pallas_call(final_kernel, in_specs=[vmem] * 2 + [hbm] * 6, out_specs=h...  7.69 us
    all_to_all x1, starting transfers between devices, shards(): entering = lax.all_to_all(entering, 'ctx', 0, 0)  5.3 us
    all_to_all x1, waiting for transfers between devices, shards(): entering = lax.all_to_all(entering, 'ctx', 0, 0)  2.17 us
    all_to_all x1, waiting for transfers between devices, shards(): received = lax.all_to_all(ends, 'ctx', 0, 0)  1.93 us
  transfers between devices with their start and end apart: 2, of which 2 were waited for; matrix products, arithmetic and copies ran while one was open for 0% of the time, Pallas kernels for 34%

profile of v4, /device:TPU:0, one launch (start us, length us, event | category | flops | bytes accessed | tf_op | source)
XLA Modules:
  0.0 56.5 jit_solution(754551273034649129)
XLA Ops:
  0.0 0.0 copy-start.2
  0.0 10.3 %end_state.1 = (bf16[16,144,128]{2,1,0:T(8,128)(2,1)}, f32[1024,2048]{1,0:T(8,128)}) custom-call(bf16[1024,2048]{1,0:T(8,128)(2,1)} %x_hbm.1, f32[4,2048]{1,0:T(4,128)} %weight_ref.1, bf16[1024,128]{1,0:T(8,128)(2,1)} %write_hbm.3, f32[32,1024]{1,0:T(8,128)} %step_hbm.3, f32[32,1024]{1,0:T(8,128)} %decay_hbm.2), custom_call_target="tpu_custom_call" | custom-call | tf_op jit(solution)/shard_map/end_state/pallas_call | solution.py:236
  10.3 8.1 %all-to-all-start = ((bf16[16,144,128]{2,1,0:T(8,128)(2,1)}), bf16[16,144,128]{2,1,0:T(8,128)(2,1)S(1)}, u32[]{:S(2)}, u32[]{:S(2)}) async-start(bf16[16,144,128]{2,1,0:T(8,128)(2,1)} %get-tuple-element.20), calls=%async_computation | async-start | bytes 1179648 | tf_op jit(solution)/shard_map/all_to_all | solution.py:676
  18.4 0.0 copy-done.2
  18.4 0.1 copy.10.skip_ref
  18.5 0.0 copy-start
  18.5 9.9 %first_local.1 = (bf16[1024,64]{1,0:T(8,128)(2,1)}, bf16[1024,64]{1,0:T(8,128)(2,1)}, bf16[1024,64]{1,0:T(8,128)(2,1)}, bf16[1024,256]{1,0:T(8,128)(2,1)}, bf16[...) custom-call(bf16[1024,128]{1,0:T(8,128)(2,1)} %write_hbm.3, bf16[1024,128]{1,0:T(8,128)(2,1)} %read_hbm.3, ...), custom_call_target="tpu_custom_call" | custom-call | tf_op jit(solution)/shard_map/first_local/pallas_call | solution.py:517
  28.4 1.9 %all-to-all-done.in_ref = bf16[16,144,128]{2,1,0:T(8,128)(2,1)S(1)} async-done(((bf16[16,144,128]{2,1,0:T(8,128)(2,1)}), bf16[16,144,128]{2,1,0:T(8,128)(2,1)S(1)}, u32[]{:S(2)}, u32[]{:S(2)}) %all-to-all-start) | async-done | bytes 589856 | tf_op jit(solution)/shard_map/all_to_all | solution.py:676
  30.3 0.0 copy-done
  30.3 1.5 %prefix.1 = bf16[16,144,128]{2,1,0:T(8,128)(2,1)} custom-call(s32[1]{0:T(128)} %bitcast.place_ref, bf16[16,144,128]{2,1,0:T(8,128)(2,1)S(1)} %all-to-all-done.in_ref, f32[4,2048]{1,0:T(4,128)S(1)} %copy-done), custom_call_target="tpu_custom_call" | custom-call | tf_op jit(solution)/shard_map/prefix/pallas_call | solution.py:312
  31.9 5.3 %all-to-all-start.1 = ((bf16[16,144,128]{2,1,0:T(8,128)(2,1)}), bf16[16,144,128]{2,1,0:T(8,128)(2,1)S(1)}, u32[]{:S(2)}, u32[]{:S(2)}) async-start(bf16[16,144,128]{2,1,0:T(8,128)(2,1)} %prefix.1), calls=%async_computation.1 | async-start | bytes 1179648 | tf_op jit(solution)/shard_map/all_to_all | solution.py:684
  37.2 0.0 copy-start.1
  37.2 9.4 %second_local.1.right_hbm = f32[1024,1024]{1,0:T(8,128)} custom-call(bf16[1024,64]{1,0:T(8,128)(2,1)} %get-tuple-element.28.gains_hbm, bf16[1024,64]{1,0:T(8,128)(2,1)} %get-tuple-element.29.fades_hbm, bf16[1024,256]{1,0:T(8,128)(2,1)} %get-tuple-element.30.keys_hbm, bf16[1024,640]{1,0:T(8,128)(2,1)} %get-tuple-element.31.mix_hbm, ...), custom_call_target="tpu_custom_call" | custom-call | tf_op jit(solution)/shard_map/second_local/pallas_call | solution.py:537
  46.6 2.2 %all-to-all-done.1.state_ref = bf16[16,144,128]{2,1,0:T(8,128)(2,1)S(1)} async-done(((bf16[16,144,128]{2,1,0:T(8,128)(2,1)}), bf16[16,144,128]{2,1,0:T(8,128)(2,1)S(1)}, u32[]{:S(2)}, u32[]{:S(2)}) %all-to-all-start.1) | async-done | bytes 589856 | tf_op jit(solution)/shard_map/all_to_all | solution.py:684
  48.8 0.0 copy-done.1
  48.8 7.7 %final_part.1 = bf16[1024,2048]{1,0:T(8,128)(2,1)} custom-call(bf16[16,144,128]{2,1,0:T(8,128)(2,1)S(1)} %all-to-all-done.1.state_ref, f32[1,2048]{1,0:T(1,128)S(1)} %bitcast.3, bf16[1024,128]{1,0:T(8,128)(2,1)} %read_hbm.3, bf16[1024,64]{1,0:T(8,128)(2,1)} %get-tuple-element.25.fade_hbm, f32[16,2048]{1,0:T(8,128)} %get-tuple-element.26.rowed_hbm, ...), custom_call_target="tpu_custom_call" | custom-call | tf_op jit(solution)/shard_map/final_part/pallas_call | solution.py:650
Async XLA Ops:
  0.0 18.4 %copy-start.2 = (f32[32]{0:T(128)S(1)}, f32[32]{0:T(128)}, u32[]{:S(2)}) copy-start(f32[32]{0:T(128)} %param.16) | copy-start | bytes 388
  10.3 20.0 %all-to-all-start = ((bf16[16,144,128]{2,1,0:T(8,128)(2,1)}), bf16[16,144,128]{2,1,0:T(8,128)(2,1)S(1)}, u32[]{:S(2)}, u32[]{:S(2)}) async-start(bf16[16,144,128]{2,1,0:T(8,128)(2,1)} %get-tuple-element.20), calls=%async_computation | async-start | bytes 1179648 | tf_op jit(solution)/shard_map/all_to_all | solution.py:676
  18.5 11.8 %copy-start = (f32[4,2048]{1,0:T(4,128)S(1)}, f32[4,2048]{1,0:T(4,128)}, u32[]{:S(2)}) copy-start(f32[4,2048]{1,0:T(4,128)} %weight_ref.1) | copy-start | bytes 98308
  31.9 16.9 %all-to-all-start.1 = ((bf16[16,144,128]{2,1,0:T(8,128)(2,1)}), bf16[16,144,128]{2,1,0:T(8,128)(2,1)S(1)}, u32[]{:S(2)}, u32[]{:S(2)}) async-start(bf16[16,144,128]{2,1,0:T(8,128)(2,1)} %prefix.1), calls=%async_computation.1 | async-start | bytes 1179648 | tf_op jit(solution)/shard_map/all_to_all | solution.py:684
  37.2 11.6 %copy-start.1 = (f32[2048]{0:T(1024)S(1)}, f32[2048]{0:T(1024)}, u32[]{:S(2)}) copy-start(f32[2048]{0:T(1024)} %param.17) | copy-start | bytes 24580

commit v5 on v4

--- a/solution.py
+++ b/solution.py
@@ -291,10 +291,20 @@
     low = (value - high.astype(F32)).astype(BF16)
     keys = jnp.where((row >= 1) & (row <= 3), tile, 0.0).reshape(count * EXTRA, 128).T.astype(BF16)
     blocks[...] = jnp.zeros(blocks.shape, BF16)
+    half = count // 2
+    depth = half * EXTRA
     for j in range(count):
-        blocks[EXTRA * j : EXTRA * (j + 1), 128 * j : 128 * (j + 1)] = high[j]
-        blocks[EXTRA * (count + j) : EXTRA * (count + j + 1), 128 * j : 128 * (j + 1)] = low[j]
-    first = dot(jnp.concatenate([keys, keys], axis=1), blocks[...])
+        side, place = divmod(j, half)
+        lanes = slice(128 * place, 128 * (place + 1))
+        start = 2 * depth * side + EXTRA * place
+        blocks[start : start + EXTRA, lanes] = high[j]
+        blocks[start + depth : start + depth + EXTRA, lanes] = low[j]
+    firsts_of = []
+    for side in range(2):
+        part = keys[:, depth * side : depth * (side + 1)]
+        both = blocks[2 * depth * side : 2 * depth * (side + 1)]
+        firsts_of.append(dot(jnp.concatenate([part, part], axis=1), both))
+    first = jnp.concatenate(firsts_of, axis=1)
     state = jnp.zeros((STATE, 128), F32)
     top_row = iota((EXTRA, 128), 0) == 0
     for j in range(count):
@@ -314,7 +324,7 @@
         in_specs=[pl.BlockSpec(memory_space=pltpu.SMEM), whole, whole],
         out_specs=whole,
         out_shape=jax.ShapeDtypeStruct(received.shape, BF16),
-        scratch_shapes=[pltpu.VMEM((2 * count * EXTRA, count * 128), BF16)],
+        scratch_shapes=[pltpu.VMEM((2 * count * EXTRA, (count // 2) * 128), BF16)],
         compiler_params=pltpu.CompilerParams(vmem_limit_bytes=VMEM_BYTES),
         name="prefix",
     )(place, received, weight)

time: 56.8 us -> 56.8 us (level)
  no operation moved by 1% of the time
where the time goes in v5:
time: 56.8 us; the launch traced here: 56.5 us
  Pallas kernels  38.8 us (68%)
  starting transfers between devices  13.4 us (24%)
  waiting for transfers between devices  4.1 us (7%)
    pallas_call x1, Pallas kernels, end_state(): pl.pallas_call(end_state_kernel, in_specs=[pl.BlockSpec(memory_space=pltp...  10.3 us
    pallas_call x1, Pallas kernels, first_local(): pl.pallas_call(functools.partial(first_kernel, 0), in_specs=[hbm] * 4 + [...  9.86 us
    pallas_call x1, Pallas kernels, second_local(): pl.pallas_call(functools.partial(second_kernel, begin), in_specs=[hbm] *...  9.44 us
    all_to_all x1, starting transfers between devices, shards(): received = lax.all_to_all(ends, 'ctx', 0, 0)  8.13 us
    pallas_call x1, Pallas kernels, final_part(): pl.pallas_call(final_kernel, in_specs=[vmem] * 2 + [hbm] * 6, out_specs=h...  7.68 us
    all_to_all x1, starting transfers between devices, shards(): entering = lax.all_to_all(entering, 'ctx', 0, 0)  5.3 us
    all_to_all x1, waiting for transfers between devices, shards(): entering = lax.all_to_all(entering, 'ctx', 0, 0)  2.17 us
    all_to_all x1, waiting for transfers between devices, shards(): received = lax.all_to_all(ends, 'ctx', 0, 0)  1.93 us
  transfers between devices with their start and end apart: 2, of which 2 were waited for; matrix products, arithmetic and copies ran while one was open for 0% of the time, Pallas kernels for 34%

profile of v5, /device:TPU:0, one launch (start us, length us, event | category | flops | bytes accessed | tf_op | source)
XLA Modules:
  0.0 56.5 jit_solution(6933613433092779108)
XLA Ops:
  0.0 0.0 copy-start.2
  0.0 10.3 %end_state.1 = (bf16[16,144,128]{2,1,0:T(8,128)(2,1)}, f32[1024,2048]{1,0:T(8,128)}) custom-call(bf16[1024,2048]{1,0:T(8,128)(2,1)} %x_hbm.1, f32[4,2048]{1,0:T(4,128)} %weight_ref.1, bf16[1024,128]{1,0:T(8,128)(2,1)} %write_hbm.3, f32[32,1024]{1,0:T(8,128)} %step_hbm.3, f32[32,1024]{1,0:T(8,128)} %decay_hbm.2), custom_call_target="tpu_custom_call" | custom-call | tf_op jit(solution)/shard_map/end_state/pallas_call | solution.py:236
  10.3 8.1 %all-to-all-start = ((bf16[16,144,128]{2,1,0:T(8,128)(2,1)}), bf16[16,144,128]{2,1,0:T(8,128)(2,1)S(1)}, u32[]{:S(2)}, u32[]{:S(2)}) async-start(bf16[16,144,128]{2,1,0:T(8,128)(2,1)} %get-tuple-element.20), calls=%async_computation | async-start | bytes 1179648 | tf_op jit(solution)/shard_map/all_to_all | solution.py:686
  18.4 0.0 copy-done.2
  18.4 0.1 copy.10.skip_ref
  18.5 0.0 copy-start
  18.5 9.9 %first_local.1 = (bf16[1024,64]{1,0:T(8,128)(2,1)}, bf16[1024,64]{1,0:T(8,128)(2,1)}, bf16[1024,64]{1,0:T(8,128)(2,1)}, bf16[1024,256]{1,0:T(8,128)(2,1)}, bf16[...) custom-call(bf16[1024,128]{1,0:T(8,128)(2,1)} %write_hbm.3, bf16[1024,128]{1,0:T(8,128)(2,1)} %read_hbm.3, ...), custom_call_target="tpu_custom_call" | custom-call | tf_op jit(solution)/shard_map/first_local/pallas_call | solution.py:527
  28.4 1.9 %all-to-all-done.in_ref = bf16[16,144,128]{2,1,0:T(8,128)(2,1)S(1)} async-done(((bf16[16,144,128]{2,1,0:T(8,128)(2,1)}), bf16[16,144,128]{2,1,0:T(8,128)(2,1)S(1)}, u32[]{:S(2)}, u32[]{:S(2)}) %all-to-all-start) | async-done | bytes 589856 | tf_op jit(solution)/shard_map/all_to_all | solution.py:686
  30.3 0.0 copy-done
  30.3 1.5 %prefix.1 = bf16[16,144,128]{2,1,0:T(8,128)(2,1)} custom-call(s32[1]{0:T(128)} %bitcast.place_ref, bf16[16,144,128]{2,1,0:T(8,128)(2,1)S(1)} %all-to-all-done.in_ref, f32[4,2048]{1,0:T(4,128)S(1)} %copy-done), custom_call_target="tpu_custom_call" | custom-call | tf_op jit(solution)/shard_map/prefix/pallas_call | solution.py:322
  31.9 5.3 %all-to-all-start.1 = ((bf16[16,144,128]{2,1,0:T(8,128)(2,1)}), bf16[16,144,128]{2,1,0:T(8,128)(2,1)S(1)}, u32[]{:S(2)}, u32[]{:S(2)}) async-start(bf16[16,144,128]{2,1,0:T(8,128)(2,1)} %prefix.1), calls=%async_computation.1 | async-start | bytes 1179648 | tf_op jit(solution)/shard_map/all_to_all | solution.py:694
  37.2 0.0 copy-start.1
  37.2 9.4 %second_local.1.right_hbm = f32[1024,1024]{1,0:T(8,128)} custom-call(bf16[1024,64]{1,0:T(8,128)(2,1)} %get-tuple-element.28.gains_hbm, bf16[1024,64]{1,0:T(8,128)(2,1)} %get-tuple-element.29.fades_hbm, bf16[1024,256]{1,0:T(8,128)(2,1)} %get-tuple-element.30.keys_hbm, bf16[1024,640]{1,0:T(8,128)(2,1)} %get-tuple-element.31.mix_hbm, ...), custom_call_target="tpu_custom_call" | custom-call | tf_op jit(solution)/shard_map/second_local/pallas_call | solution.py:547
  46.6 2.2 %all-to-all-done.1.state_ref = bf16[16,144,128]{2,1,0:T(8,128)(2,1)S(1)} async-done(((bf16[16,144,128]{2,1,0:T(8,128)(2,1)}), bf16[16,144,128]{2,1,0:T(8,128)(2,1)S(1)}, u32[]{:S(2)}, u32[]{:S(2)}) %all-to-all-start.1) | async-done | bytes 589856 | tf_op jit(solution)/shard_map/all_to_all | solution.py:694
  48.8 0.0 copy-done.1
  48.8 7.7 %final_part.1 = bf16[1024,2048]{1,0:T(8,128)(2,1)} custom-call(bf16[16,144,128]{2,1,0:T(8,128)(2,1)S(1)} %all-to-all-done.1.state_ref, f32[1,2048]{1,0:T(1,128)S(1)} %bitcast.3, bf16[1024,128]{1,0:T(8,128)(2,1)} %read_hbm.3, bf16[1024,64]{1,0:T(8,128)(2,1)} %get-tuple-element.25.fade_hbm, f32[16,2048]{1,0:T(8,128)} %get-tuple-element.26.rowed_hbm, ...), custom_call_target="tpu_custom_call" | custom-call | tf_op jit(solution)/shard_map/final_part/pallas_call | solution.py:660
Async XLA Ops:
  0.0 18.4 %copy-start.2 = (f32[32]{0:T(128)S(1)}, f32[32]{0:T(128)}, u32[]{:S(2)}) copy-start(f32[32]{0:T(128)} %param.16) | copy-start | bytes 388
  10.3 20.0 %all-to-all-start = ((bf16[16,144,128]{2,1,0:T(8,128)(2,1)}), bf16[16,144,128]{2,1,0:T(8,128)(2,1)S(1)}, u32[]{:S(2)}, u32[]{:S(2)}) async-start(bf16[16,144,128]{2,1,0:T(8,128)(2,1)} %get-tuple-element.20), calls=%async_computation | async-start | bytes 1179648 | tf_op jit(solution)/shard_map/all_to_all | solution.py:686
  18.5 11.8 %copy-start = (f32[4,2048]{1,0:T(4,128)S(1)}, f32[4,2048]{1,0:T(4,128)}, u32[]{:S(2)}) copy-start(f32[4,2048]{1,0:T(4,128)} %weight_ref.1) | copy-start | bytes 98308
  31.9 16.9 %all-to-all-start.1 = ((bf16[16,144,128]{2,1,0:T(8,128)(2,1)}), bf16[16,144,128]{2,1,0:T(8,128)(2,1)S(1)}, u32[]{:S(2)}, u32[]{:S(2)}) async-start(bf16[16,144,128]{2,1,0:T(8,128)(2,1)} %prefix.1), calls=%async_computation.1 | async-start | bytes 1179648 | tf_op jit(solution)/shard_map/all_to_all | solution.py:694
  37.2 11.6 %copy-start.1 = (f32[2048]{0:T(1024)S(1)}, f32[2048]{0:T(1024)}, u32[]{:S(2)}) copy-start(f32[2048]{0:T(1024)} %param.17) | copy-start | bytes 24580
